TPU v7x, 32 devices: a whole 2x2x4 slice. The times are simulated.
32 devices in a mesh: seq: 8 (over z, x), fsdp: 4 (over y, core).
Axes of the slice: x: 2, y: 2, z: 4, core: 2. Of those that a mesh axis runs over, the one named last changes fastest.
Arguments:
- projected: bfloat16 [3, 8192, 4096], P(None, 'fsdp', 'seq'), may hold values from -6 to 6
- short_weight: float32 [3, 8192, 3], P(None, 'fsdp'), may hold values from -3.5 to 3.5
- skip_weight: float32 [8192], P('fsdp'), may hold values from -4 to 4
- decay_rates: float32 [8192, 16], P('fsdp'), may hold values from 0.00012207031 to 0.05
- residues: float32 [8192, 16], P('fsdp'), may hold values from -1.5 to 1.5
Outputs:
- output: bfloat16 [8192, 4096], P('fsdp', 'seq')
All inputs are finite; a program needn't handle non-finite values.
Results may differ from a plain program's by a relative error of at most 0.0058.
Values may be sent and summed in bfloat16 or wider, within the bound.
A program may use at most 128 MiB of HBM per device.

v0:
```python
import math

import jax
import jax.numpy as jnp
from jax import lax
from jax.sharding import PartitionSpec as P


def from_behind(value, axis, steps):
    count = lax.axis_size(axis)
    leading, last = (max(0, -steps), min(count, count - steps))
    return lax.ppermute(value, axis, [(source, source + steps) for source in range(leading, last)])


def combine(earlier, later):
    return (earlier[0] * later[0], later[0] * earlier[1] + later[1])


def modal_block(signal, weight, decay_rate, initial):
    channels, length = signal.shape
    block_len = min(128, length)
    block_count = length // block_len
    offsets = jnp.arange(block_len, dtype=jnp.float32)
    falloff = jnp.exp(-decay_rate[:, :, None] * offsets)
    filter_taps = jnp.einsum("gk,gkb->gb", weight, falloff, precision=lax.Precision.HIGHEST)
    positions = jnp.arange(block_len, dtype=jnp.int32)
    lag_index = positions[:, None] - positions[None, :]
    toeplitz = jnp.where(lag_index >= 0, filter_taps[:, jnp.maximum(lag_index, 0)], 0.0)
    sliced = signal.reshape(channels, block_count, block_len)
    inside = jnp.einsum("gij,gnj->gni", toeplitz, sliced, precision=lax.Precision.HIGHEST)
    entering = jnp.exp(-decay_rate[:, :, None] * (block_len - offsets))
    block_ends = jnp.einsum("gkj,gnj->gkn", entering, sliced, precision=lax.Precision.HIGHEST)
    decays = jnp.broadcast_to(jnp.exp(-decay_rate * block_len)[:, :, None], block_ends.shape)
    powers, partial_sums = lax.associative_scan(combine, (decays, block_ends), axis=2)
    states_after = powers * initial[:, :, None] + partial_sums
    states = jnp.concatenate([initial[:, :, None], states_after[:, :, :-1]], axis=2)
    carried = jnp.einsum(
        "gkb,gkn->gnb", weight[:, :, None] * falloff, states, precision=lax.Precision.HIGHEST
    )
    return ((inside + carried).reshape(channels, length), states_after[:, :, -1])


def grouped(signal, weight, decay_rate, initial):
    channels, length = signal.shape
    group = math.gcd(channels, 64)
    count = channels // group
    pieces = (
        signal.reshape(count, group, length),
        weight.reshape(count, group, -1),
        decay_rate.reshape(count, group, -1),
        initial.reshape(count, group, -1),
    )

    def apply_one(item):
        return modal_block(item[0], item[1], item[2], item[3])

    results, finals = lax.map(apply_one, pieces)
    return (results.reshape(channels, length), finals.reshape(channels, -1))


def shards(projected, short_weight, skip_weight, decay_rates, residues):
    taps_count = short_weight.shape[2]
    channels = projected.shape[1]
    length = projected.shape[2]
    tail = jnp.swapaxes(projected[:, :, length - (taps_count - 1) :], 1, 2)
    before = from_behind(tail, "seq", 1)
    padded = jnp.concatenate([jnp.swapaxes(before, 1, 2), projected], axis=2).astype(jnp.float32)
    feats = jnp.zeros((3, channels, length), jnp.float32)
    for lag in range(taps_count):
        begin = taps_count - 1 - lag
        feats = feats + short_weight[:, :, lag][:, :, None] * padded[:, :, begin : begin + length]
    mixed = (feats[1] * feats[2]).astype(jnp.bfloat16)
    mixed = lax.optimization_barrier(mixed)
    owned = channels // lax.axis_size("seq")
    first = lax.axis_index("seq") * owned
    decay_rate = lax.dynamic_slice_in_dim(decay_rates, first, owned, 0)
    residue = lax.dynamic_slice_in_dim(residues, first, owned, 0)
    weight = residue * jnp.sqrt(2.0 * decay_rate)
    gains = lax.dynamic_slice_in_dim(skip_weight, first, owned, 0)
    regrouped = lax.all_to_all(mixed, "seq", split_axis=0, concat_axis=1, tiled=True)
    signal = regrouped.astype(jnp.float32)
    zeros_state = jnp.zeros(decay_rate.shape, jnp.float32)
    convolved, unused = grouped(signal, weight, decay_rate, zeros_state)
    summed = (convolved + gains[:, None] * signal).astype(jnp.bfloat16)
    summed = lax.all_to_all(summed, "seq", split_axis=1, concat_axis=0, tiled=True)
    return (feats[0] * summed.astype(jnp.float32)).astype(jnp.bfloat16)


def solution(mesh):
    return jax.shard_map(
        shards,
        mesh=mesh,
        in_specs=(
            P(None, "fsdp", "seq"),
            P(None, "fsdp", None),
            P("fsdp"),
            P("fsdp", None),
            P("fsdp", None),
        ),
        out_specs=P("fsdp", "seq"),
        check_vma=False,
    )
```

profile of v0, /device:TPU:28, one launch (start us, length us, event | category | flops | bytes accessed | tf_op | source)
XLA Modules:
  0.0 531.7 jit_solution(1661453066978865274)
XLA Ops:
  2.7 3.4 collective-permute-start
  6.2 3.1 collective-permute-done
  10.1 11.7 %maximum_convert_fusion = f32[3,2048,514]{2,1,0:T(8,128)} fusion(bf16[3,2048,512]{2,1,0:T(8,128)(2,1)} %param.7, bf16[3,2048,2]{2,1,0:T(8,128)(2,1)S(1)} %copy.124), kind=kLoop, calls=%fused_computation.79 | loop fusion | flops 12632064 | bytes 18948096 | tf_op jit(solution)/shard_map/convert_element_type | solution.py:67
  21.8 17.6 %fusion.33 = f32[3,2048,512]{2,1,0:T(8,128)S(1)} fusion(f32[3,2048,514]{2,1,0:T(8,128)} %maximum_convert_fusion, f32[3,2048]{1,0:T(4,128)S(1)} %get-tuple-element.94, f32[3,2048]{1,0:T(4,128)S(1)} %get-tuple-element.95, f32[3,2048]{1,0:T(4,128)S(1)} %bitcast.133), kind=kLoop, calls=%fused_computation.75 | loop fusion | flops 15728640 | bytes 50405376 | tf_op jit(solution)/shard_map/add | solution.py:71
  39.4 4.5 copy-done
  46.0 5.1 all-to-all-start
  52.8 42.9 %all-to-all-done = bf16[8,256,512]{2,1,0:T(8,128)(2,1)S(1)} async-done(((bf16[8,256,512]{2,1,0:T(8,128)(2,1)}), bf16[8,256,512]{2,1,0:T(8,128)(2,1)S(1)}, u32[]{:S(2)}, u32[]{:S(2)}) %all-to-all-start) | async-done | bytes 2097184 | tf_op jit(solution)/shard_map/all_to_all | solution.py:80
  96.3 4.4 copy.125
  100.7 5.0 reshape.128
  105.7 361.2 %while.10 = (s32[]{:T(128)}, f32[4,64,4096]{2,1,0:T(8,128)}, f32[4,64,4096]{2,1,0:T(8,128)}, f32[4,64,16]{2,1,0:T(8,128)S(1)}, f32[4,64,16]{1,0,2:T(4,128)S(1)}, /*index=5*/s32[]{:T(128)}, f32[]{:T(128)}) while((s32[]{:T(128)}, f32[4,64,4096]{2,1,0:T(8,128)}, f32[4,64,4096]{2,1,0:T(8,128)}, f32[4,64,16]{2,1,0:T(8,128)S(1)}, ...), condition=%wide.region_1.2_spmd, body=%wide.region_0.1_spmd.sunk | while | flops 507272320 | bytes 40769180 | solution.py:57
  109.1 3.2 slice.331
  112.6 3.0 slice.332
  124.6 54.4 %gather_fusion = f32[16384,64]{1,0:T(8,128)} fusion(f32[64,128]{0,1:T(8,128)S(1)} %bitcast.119, s32[16384]{0:T(1024)S(1)} %bitcast_clamp_fusion.2), kind=kCustom, calls=%fused_computation.clone.1 | custom fusion | bytes 8454144 | tf_op jit(solution)/shard_map/while/body/eval_jaxpr/gather | solution.py:28
  179.0 7.3 %copy.165 = f32[128,128,64]{1,0,2:T(8,128)} copy(f32[128,128,64]{2,1,0:T(8,128)} %bitcast.120) | data formatting | bytes 8388608 | tf_op jit(solution)/shard_map/while/body/eval_jaxpr/gather | solution.py:28
  186.4 8.3 %fusion.73 = f32[64,32,128]{2,1,0:T(8,128)S(1)} fusion(f32[64,32,128]{2,1,0:T(8,128)S(1)} %fusion.71, f32[64,32,128]{2,1,0:T(8,128)S(1)} %bitcast.123, f32[128,128,64]{1,0,2:T(8,128)} %copy.165, pred[128,128]{1,0:T(8,128)(4,1)S(1)} %subtract_compare_fusion.2), kind=kOutput, calls=%fused_computation.6.clone.1 | convolution fusion | flops 403963904 | bytes 7356416 | tf_op jit(solution)/shard_map/while/body/eval_jaxpr/gij,gnj->gni/dot_general | solution.py:30
  199.5 3.2 slice.331
  202.9 3.0 slice.332
  215.0 54.4 %gather_fusion = f32[16384,64]{1,0:T(8,128)} fusion(f32[64,128]{0,1:T(8,128)S(1)} %bitcast.119, s32[16384]{0:T(1024)S(1)} %bitcast_clamp_fusion.2), kind=kCustom, calls=%fused_computation.clone.1 | custom fusion | bytes 8454144 | tf_op jit(solution)/shard_map/while/body/eval_jaxpr/gather | solution.py:28
  269.3 7.3 %copy.165 = f32[128,128,64]{1,0,2:T(8,128)} copy(f32[128,128,64]{2,1,0:T(8,128)} %bitcast.120) | data formatting | bytes 8388608 | tf_op jit(solution)/shard_map/while/body/eval_jaxpr/gather | solution.py:28
  276.7 8.3 %fusion.73 = f32[64,32,128]{2,1,0:T(8,128)S(1)} fusion(f32[64,32,128]{2,1,0:T(8,128)S(1)} %fusion.71, f32[64,32,128]{2,1,0:T(8,128)S(1)} %bitcast.123, f32[128,128,64]{1,0,2:T(8,128)} %copy.165, pred[128,128]{1,0:T(8,128)(4,1)S(1)} %subtract_compare_fusion.2), kind=kOutput, calls=%fused_computation.6.clone.1 | convolution fusion | flops 403963904 | bytes 7356416 | tf_op jit(solution)/shard_map/while/body/eval_jaxpr/gij,gnj->gni/dot_general | solution.py:30
  289.7 3.2 slice.331
  293.2 3.0 slice.332
  305.2 54.4 %gather_fusion = f32[16384,64]{1,0:T(8,128)} fusion(f32[64,128]{0,1:T(8,128)S(1)} %bitcast.119, s32[16384]{0:T(1024)S(1)} %bitcast_clamp_fusion.2), kind=kCustom, calls=%fused_computation.clone.1 | custom fusion | bytes 8454144 | tf_op jit(solution)/shard_map/while/body/eval_jaxpr/gather | solution.py:28
  359.6 7.3 %copy.165 = f32[128,128,64]{1,0,2:T(8,128)} copy(f32[128,128,64]{2,1,0:T(8,128)} %bitcast.120) | data formatting | bytes 8388608 | tf_op jit(solution)/shard_map/while/body/eval_jaxpr/gather | solution.py:28
  367.0 8.3 %fusion.73 = f32[64,32,128]{2,1,0:T(8,128)S(1)} fusion(f32[64,32,128]{2,1,0:T(8,128)S(1)} %fusion.71, f32[64,32,128]{2,1,0:T(8,128)S(1)} %bitcast.123, f32[128,128,64]{1,0,2:T(8,128)} %copy.165, pred[128,128]{1,0:T(8,128)(4,1)S(1)} %subtract_compare_fusion.2), kind=kOutput, calls=%fused_computation.6.clone.1 | convolution fusion | flops 403963904 | bytes 7356416 | tf_op jit(solution)/shard_map/while/body/eval_jaxpr/gij,gnj->gni/dot_general | solution.py:30
  380.0 3.2 slice.331
  395.5 54.4 %gather_fusion = f32[16384,64]{1,0:T(8,128)} fusion(f32[64,128]{0,1:T(8,128)S(1)} %bitcast.119, s32[16384]{0:T(1024)S(1)} %bitcast_clamp_fusion.2), kind=kCustom, calls=%fused_computation.clone.1 | custom fusion | bytes 8454144 | tf_op jit(solution)/shard_map/while/body/eval_jaxpr/gather | solution.py:28
  449.9 7.3 %copy.165 = f32[128,128,64]{1,0,2:T(8,128)} copy(f32[128,128,64]{2,1,0:T(8,128)} %bitcast.120) | data formatting | bytes 8388608 | tf_op jit(solution)/shard_map/while/body/eval_jaxpr/gather | solution.py:28
  457.2 8.3 %fusion.73 = f32[64,32,128]{2,1,0:T(8,128)S(1)} fusion(f32[64,32,128]{2,1,0:T(8,128)S(1)} %fusion.71, f32[64,32,128]{2,1,0:T(8,128)S(1)} %bitcast.123, f32[128,128,64]{1,0,2:T(8,128)} %copy.165, pred[128,128]{1,0:T(8,128)(4,1)S(1)} %subtract_compare_fusion.2), kind=kOutput, calls=%fused_computation.6.clone.1 | convolution fusion | flops 403963904 | bytes 7356416 | tf_op jit(solution)/shard_map/while/body/eval_jaxpr/gij,gnj->gni/dot_general | solution.py:30
  466.8 6.1 %copy.142 = f32[32,8,8,512]{3,2,1,0:T(8,128)S(1)} copy(f32[32,8,8,512]{3,1,2,0:T(8,128)} %bitcast.130) | data formatting | bytes 8388608
  475.7 51.6 %all_to_all.23 = bf16[256,8,512]{2,0,1:T(8,128)(2,1)S(1)} all-to-all(bf16[256,8,512]{2,0,1:T(8,128)(2,1)S(1)} %fusion.37), channel_id=1, replica_groups=mesh['seq'=8,'fsdp'=4] {'seq'}, dimensions={1} | all-to-all | bytes 4194304 | tf_op jit(solution)/shard_map/all_to_all | solution.py:85
  527.3 4.4 fusion.40
  (282 shorter events, 68.2 us)
Async XLA Ops:
  0.0 6.1 %copy-start.3 = (f32[3,2048,3]{1,2,0:T(4,128)S(1)}, f32[3,2048,3]{1,2,0:T(4,128)}, u32[]{:S(2)}) copy-start(f32[3,2048,3]{1,2,0:T(4,128)} %param.8) | copy-start | bytes 221188
  2.7 6.6 %collective-permute-start = (bf16[3,2,2048]{2,1,0:T(2,128)(2,1)S(1)}, bf16[3,2,2048]{2,1,0:T(2,128)(2,1)S(1)}, u32[]{:S(2)}, u32[]{:S(2)}) collective-permute-start(bf16[3,2,2048]{2,1,0:T(2,128)(2,1)S(1)} %bitcast.134), channel_id=1, source_target_pairs={{0,4},{4,8},{8,12},{12,16},{16,20},{20,24},{24,28},{1,5},{5,9},{9,... | collective-permute-start | bytes 73736 | tf_op jit(solution)/shard_map/ppermute | solution.py:12
  39.4 4.5 copy-start
  46.0 49.8 %all-to-all-start = ((bf16[8,256,512]{2,1,0:T(8,128)(2,1)}), bf16[8,256,512]{2,1,0:T(8,128)(2,1)S(1)}, u32[]{:S(2)}, u32[]{:S(2)}) async-start(bf16[8,256,512]{2,1,0:T(8,128)(2,1)} %bitcast.125), calls=%async_computation | async-start | bytes 4194304 | tf_op jit(solution)/shard_map/all_to_all | solution.py:80
  95.7 4.9 copy-start.1
  466.8 6.1 %copy-start.2 = (bf16[8,256,512]{2,1,0:T(8,128)(2,1)S(1)}, bf16[8,256,512]{2,1,0:T(8,128)(2,1)}, u32[]{:S(2)}) copy-start(bf16[8,256,512]{2,1,0:T(8,128)(2,1)} %copy-done.1) | copy-start | bytes 6291460
where the time goes:
time: 536 us; the launch traced here: 532 us
  local copies, waits for them, and re-layouts  330 us (62%)
  matrix products  52.4 us (10%)
  blocking collectives  51.6 us (10%)
  waiting for transfers between devices  46 us (9%)
  other arithmetic  41.4 us (8%)
  starting transfers between devices  8.53 us (2%)
    gather x8, local copies, waits for them, and re-layouts, modal_block(): filter_taps[:, jnp.maximum(lag_index, 0)]  247 us
    all_to_all x1, blocking collectives, shards(): lax.all_to_all(summed, 'seq', split_axis=1, concat_axis=0, tiled=True)  51.6 us
    all_to_all x1, waiting for transfers between devices, shards(): lax.all_to_all(mixed, 'seq', split_axis=0, concat_axis=1, tiled=True)  42.9 us
    slice x20, local copies, waits for them, and re-layouts, modal_block(): lax.associative_scan(combine, (decays, block_ends), axis=2)  36.9 us
    dot_general x4, matrix products, modal_block(): jnp.einsum('gij,gnj->gni', toeplitz, sliced, precision=lax.Precision.HIGH...  33.3 us
    add x1, other arithmetic, shards(): feats + short_weight[:, :, lag][:, :, None] * padded[:, :, begin:begin +...  17.6 us
    while x36, local copies, waits for them, and re-layouts  12.7 us
    convert_element_type x1, other arithmetic, shards(): jnp.concatenate([jnp.swapaxes(before, 1, 2), projected], axis=2)  11.7 us
  transfers between devices with their start and end apart: 2, of which 2 were waited for; matrix products, arithmetic and copies ran while one was open for 0% of the time, Pallas kernels for 0%

commit v1 on v0

v1 whole, which is shorter than its diff:
```python
import functools

import jax
import jax.numpy as jnp
import numpy as np
from jax import lax
from jax.experimental import pallas as pl
from jax.experimental.pallas import tpu as pltpu
from jax.sharding import PartitionSpec as P

BL = 128
NB = 16
HALF = 0.025


def split(m):
    hi = m.astype(jnp.bfloat16)
    return hi, (m - np.asarray(hi, np.float64)).astype(jnp.bfloat16)


@functools.cache
def tables():
    nodes = 64
    theta = (np.arange(nodes) + 0.5) * np.pi / nodes
    t = np.arange(BL + 1)
    f = np.exp(-HALF * (1 + np.cos(theta))[:, None] * t[None, :])
    psi = np.stack(
        [(2.0 if n else 1.0) / nodes * (np.cos(n * theta) @ f) for n in range(NB)]
    )
    half = BL // 2
    ang = np.pi * np.outer(np.arange(BL), 2 * np.arange(half) + 1) / BL
    c, s = np.cos(ang), np.sin(ang)
    z = np.zeros_like(c)
    fwd = np.block([[c, z, -s, z], [z, c, z, -s]])
    inv = np.block([[c, z, -s, z], [z, c, z, -s]]).T * (2.0 / BL)
    spec = np.concatenate([psi[:, :BL] @ c] * 2 + [-psi[:, :BL] @ s] * 2, axis=1)
    unit = np.concatenate([np.ones((1, BL)), np.zeros((1, BL))], axis=1)
    spec = np.concatenate([spec, unit, np.zeros((15, 2 * BL))], axis=0)
    rev = psi[:, BL - 1 :: -1][:, :BL]
    zr = np.zeros_like(rev)
    mom = np.block([[rev, zr], [zr, rev]])
    nxt = psi[:, 1 : BL + 1]
    car = np.block([[nxt, zr], [zr, nxt]])
    sh, sl = split(spec)
    mh, ml = split(mom)
    ch, cl = split(car)
    sel = np.zeros((8, 6 * 128))
    for i in range(3):
        sel[2 * i + 1, (2 * i) * 128] = 1
        sel[2 * i, (2 * i + 1) * 128] = 1
        sel[2 * i + 1, (2 * i + 1) * 128 + 1] = 1
    cat = lambda *a: np.concatenate(a, axis=0)
    b16 = lambda a: a.astype(jnp.bfloat16)
    return dict(
        fwd=b16(fwd), inv=b16(inv), spec=cat(sh, sh, sl), mom=cat(mh, ml),
        car=cat(ch, ch, cl), sel=b16(sel),
    )


def rowdot(a, b):
    return lax.dot_general(a, b, (((0,), (0,)), ((), ())), preferred_element_type=jnp.float32)


def three(m):
    hi = m.astype(jnp.bfloat16)
    lo = (m - hi.astype(jnp.float32)).astype(jnp.bfloat16)
    return jnp.concatenate([hi, lo, hi], axis=0)


def dot(a, b):
    return jnp.dot(a, b, preferred_element_type=jnp.float32)


def feat(x, w, h1, h2):
    lane = lax.broadcasted_iota(jnp.int32, (x.shape[0], 128), 1)
    w0, w1, w2 = (w[:, i : i + 1] for i in range(3))
    out = []
    for i in range(x.shape[1] // 128):
        c = x[:, i * 128 : (i + 1) * 128].astype(jnp.float32)
        r1, r2 = pltpu.roll(c, 1, 1), pltpu.roll(c, 2, 1)
        out.append(w0 * c + w1 * jnp.where(lane < 1, h1, r1) + w2 * jnp.where(lane < 2, h2, r2))
        h1, h2 = r1, r2
    return out


ROWS = 32


def front(p_ref, halo_ref, w_ref, cheb_ref, decay_ref, sel_ref, mom_ref,
          mixed_ref, ends_ref, last_ref, hr_ref):
    tile = p_ref.shape[1]
    hr_ref[...] = rowdot(halo_ref[...], sel_ref[...])

    @pl.loop(0, tile // ROWS)
    def _(r):
        rows = pl.ds(pl.multiple_of(r * ROWS, ROWS), ROWS)
        k = feat(p_ref[1, rows, :], w_ref[1, rows, :], hr_ref[rows, 256:384], hr_ref[rows, 384:512])
        v = feat(p_ref[2, rows, :], w_ref[2, rows, :], hr_ref[rows, 512:640], hr_ref[rows, 640:768])
        for i in range(len(k)):
            mixed_ref[rows, i * 128 : (i + 1) * 128] = (k[i] * v[i]).astype(jnp.bfloat16)

    step = jnp.exp(-BL * decay_ref[...])
    total = None
    for pair in range(p_ref.shape[2] // 256):
        m = lax.dot_general(
            mom_ref[...], mixed_ref[:, pair * 256 : (pair + 1) * 256],
            (((1,), (1,)), ((), ())), preferred_element_type=jnp.float32)
        m = m[:32] + m[32:]
        for b in range(2):
            e = cheb_ref[0:16] * m[b * 16 : b * 16 + 1]
            for n in range(1, NB):
                e = e + cheb_ref[n * 16 : n * 16 + 16] * m[b * 16 + n : b * 16 + n + 1]
            ends_ref[(pair * 2 + b) * 16 : (pair * 2 + b + 1) * 16] = e
            total = e if total is None else step * total + e
    last_ref[...] = total.astype(last_ref.dtype)


def back(q_ref, mixed_ref, halo_ref, w_ref, cheb_ref, decay_ref, weight_ref, skip_ref, ends_ref, init_ref,
         sel_ref, fwd_ref, inv_ref, spec_ref, car_ref,
         out_ref, hr_ref, h_ref, y_ref):
    tile = mixed_ref.shape[0]
    hr_ref[...] = rowdot(halo_ref[...], sel_ref[:, :256])
    step = jnp.exp(-BL * decay_ref[...])
    fold = 1.0 / (1.0 + step)
    weight = weight_ref[...]
    wv = weight * fold
    g = [jnp.sum(wv * cheb_ref[n * 16 : n * 16 + 16], axis=0, keepdims=True) for n in range(NB)]
    g = jnp.concatenate(g + [skip_ref[...], jnp.zeros((15, tile), jnp.float32)], axis=0)
    h_ref[...] = rowdot(three(g), spec_ref[...])
    state = init_ref[...]
    for pair in range(mixed_ref.shape[1] // 256):
        c = []
        for b in range(2):
            e = ends_ref[(pair * 2 + b) * 16 : (pair * 2 + b + 1) * 16]
            p = weight * (state + fold * e)
            state = step * state + e
            c += [jnp.sum(p * cheb_ref[n * 16 : n * 16 + 16], axis=0, keepdims=True) for n in range(NB)]
        cols = slice(pair * 256, pair * 256 + 256)
        carried = rowdot(three(jnp.concatenate(c, axis=0)), car_ref[...])
        x = dot(mixed_ref[:, cols], fwd_ref[...])
        xr, xi = x[:, :128], x[:, 128:]
        hr, hi = h_ref[:, :128], h_ref[:, 128:]
        y = jnp.concatenate([xr * hr - xi * hi, xr * hi + xi * hr], axis=1).astype(jnp.bfloat16)
        y_ref[:, cols] = (carried + dot(y, inv_ref[...])).astype(jnp.bfloat16)

    @pl.loop(0, tile // ROWS)
    def _(r):
        rows = pl.ds(pl.multiple_of(r * ROWS, ROWS), ROWS)
        q = feat(q_ref[0, rows, :], w_ref[0, rows, :], hr_ref[rows, 0:128], hr_ref[rows, 128:256])
        for i in range(len(q)):
            cols = slice(i * 128, i * 128 + 128)
            out_ref[rows, cols] = (q[i] * y_ref[rows, cols].astype(jnp.float32)).astype(jnp.bfloat16)


def shards(projected, short_weight, skip_weight, decay_rates, residues):
    channels, length = projected.shape[1:]
    n = lax.axis_size("seq")
    me = lax.axis_index("seq")
    tab = {k: jnp.asarray(v) for k, v in tables().items()}
    tile = min(256, channels)
    blocks = length // BL
    tail = jnp.swapaxes(projected[:, :, length - 2 :], 1, 2)
    halo = lax.ppermute(tail, "seq", [(i, i + 1) for i in range(n - 1)])
    halo = jnp.pad(halo.reshape(6, channels), ((0, 2), (0, 0)))
    decay = decay_rates.T
    weight = residues.T * jnp.sqrt(2.0 * decay)
    xi = decay / HALF - 1.0
    cheb = [jnp.ones_like(xi), xi]
    for _ in range(NB - 2):
        cheb.append(2.0 * xi * cheb[-1] - cheb[-2])
    cheb = jnp.concatenate(cheb, axis=0)

    full = lambda a: pl.BlockSpec(a.shape, lambda i: (0,) * a.ndim)
    lanes = lambda r: pl.BlockSpec((r, tile), lambda i: (0, i))
    rows = pl.BlockSpec((tile, length), lambda i: (i, 0))
    params = pltpu.CompilerParams(vmem_limit_bytes=40 * 2**20)
    pspec = pl.BlockSpec((3, tile, length), lambda i: (0, i, 0))
    qspec = pl.BlockSpec((1, tile, length), lambda i: (0, i, 0))
    wspec = pl.BlockSpec((3, tile, 3), lambda i: (0, i, 0))
    mixed, ends, last = pl.pallas_call(
        front,
        grid=(channels // tile,),
        in_specs=[pspec, lanes(8), wspec, lanes(NB * 16), lanes(16), full(tab["sel"]), full(tab["mom"])],
        out_specs=[rows, lanes(blocks * 16), lanes(16)],
        out_shape=[
            jax.ShapeDtypeStruct((channels, length), jnp.bfloat16),
            jax.ShapeDtypeStruct((blocks * 16, channels), jnp.float32),
            jax.ShapeDtypeStruct((16, channels), jnp.bfloat16),
        ],
        scratch_shapes=[pltpu.VMEM((tile, 768), jnp.float32)],
        compiler_params=params,
        name="front",
    )(projected, halo, short_weight, cheb, decay, tab["sel"], tab["mom"])
    every = lax.all_gather(last, "seq")
    whole_step = jnp.exp(-length * decay)
    init = jnp.zeros((16, channels), jnp.float32)
    for i in range(n - 1):
        init = jnp.where(i < me, whole_step * init + every[i].astype(jnp.float32), init)
    return pl.pallas_call(
        back,
        grid=(channels // tile,),
        in_specs=[qspec, rows, lanes(8), wspec, lanes(NB * 16), lanes(16), lanes(16), lanes(1),
                  lanes(blocks * 16), lanes(16)]
        + [full(tab[k]) for k in ("sel", "fwd", "inv", "spec", "car")],
        out_specs=rows,
        out_shape=jax.ShapeDtypeStruct((channels, length), jnp.bfloat16),
        scratch_shapes=[
            pltpu.VMEM((tile, 256), jnp.float32),
            pltpu.VMEM((tile, 256), jnp.float32),
            pltpu.VMEM((tile, length), jnp.bfloat16),
        ],
        compiler_params=params,
        name="back",
    )(projected, mixed, halo, short_weight, cheb, decay, weight, skip_weight[None], ends, init,
      *[tab[k] for k in ("sel", "fwd", "inv", "spec", "car")])


def solution(mesh):
    return jax.shard_map(
        shards,
        mesh=mesh,
        in_specs=(
            P(None, "fsdp", "seq"),
            P(None, "fsdp", None),
            P("fsdp"),
            P("fsdp", None),
            P("fsdp", None),
        ),
        out_specs=P("fsdp", "seq"),
        check_vma=False,
    )
```

time: 536 us -> 77.7 us (0.14)
  the two profiles are of different devices: /device:TPU:28 before, /device:TPU:0 now
where the time goes in v1:
time: 77.7 us; the launch traced here: 77.4 us
  blocking collectives  31.9 us (41%)
  Pallas kernels  29.5 us (38%)
  local copies, waits for them, and re-layouts  9.47 us (12%)
  starting transfers between devices  4.98 us (6%)
  other arithmetic  1.33 us (2%)
    all_gather x1, blocking collectives, shards(): every = lax.all_gather(last, 'seq')  31.9 us
    pallas_call x1, Pallas kernels, shards(): pl.pallas_call(front, grid=(channels // tile,), in_specs=[pspec, lanes(8)...  14.9 us
    pallas_call x1, Pallas kernels, shards(): pl.pallas_call(back, grid=(channels // tile,), in_specs=[qspec, rows, lan...  14.6 us
    unnamed x31, local copies, waits for them, and re-layouts  7.51 us
    ppermute x1, starting transfers between devices, shards(): halo = lax.ppermute(tail, 'seq', [(i, i + 1) for i in range(n - 1)])  4.98 us
    slice x1, local copies, waits for them, and re-layouts, shards(): tail = jnp.swapaxes(projected[:, :, length - 2:], 1, 2)  1.93 us
  transfers between devices with their start and end apart: 1, of which 0 were waited for; matrix products, arithmetic and copies ran while one was open for 3% of the time, Pallas kernels for 0%

profile of v1, /device:TPU:0, one launch (start us, length us, event | category | flops | bytes accessed | tf_op | source)
XLA Modules:
  0.0 77.4 jit_solution(558383864224146702)
XLA Ops:
  0.0 1.9 %slice.24 = bf16[3,2048,2]{2,1,0:T(8,128)(2,1)S(1)} slice(bf16[3,2048,512]{2,1,0:T(8,128)(2,1)} %q_ref.1), slice={[0:3], [0:2048], [510:512]} | slice | bytes 49152 | tf_op jit(solution)/shard_map/slice | solution.py:162
  1.9 0.7 copy.18
  2.7 0.0 copy-start.13
  2.7 5.0 %collective-permute-start = (bf16[3,2,2048]{2,1,0:T(2,128)(2,1)S(1)}, bf16[3,2,2048]{2,1,0:T(2,128)(2,1)S(1)}, u32[]{:S(2)}, u32[]{:S(2)}) collective-permute-start(bf16[3,2,2048]{2,1,0:T(2,128)(2,1)S(1)} %bitcast.89), channel_id=1, source_target_pairs={{0,4},{4,8},{8,12},{12,16},{16,20},{20,24},{24,28},{1,5},{5,9},{9,... | collective-permute-start | bytes 73736 | tf_op jit(solution)/shard_map/ppermute | solution.py:163
  7.8 0.1 constant_dynamic-update-slice_fusion.2
  7.9 0.1 constant_dynamic-update-slice_fusion.1
  8.0 0.1 fusion.14
  8.0 0.1 fusion.13
  8.1 0.1 fusion.12
  8.2 0.1 fusion.11
  8.3 0.1 fusion.15
  8.4 0.1 fusion.10
  8.5 0.0 copy-start.7
  8.5 0.0 copy-start.10
  8.6 0.1 constant_dynamic-update-slice_fusion
  8.7 0.1 fusion.9
  8.8 0.1 subtract_dynamic-update-slice_fusion.cheb_ref
  9.0 0.0 copy-start.2
  9.0 1.3 %copy-done.2 = f32[256,2048]{1,0:T(8,128)} copy-done((f32[256,2048]{1,0:T(8,128)}, f32[256,2048]{1,0:T(8,128)S(1)}, u32[]{:S(2)}) %copy-start.2) | copy-done | bytes 2097176
  10.3 1.0 %copy.16.w_ref = f32[3,2048,3]{2,1,0:T(8,128)S(1)} copy(f32[3,2048,3]{1,2,0:T(4,128)S(1)} %copy-done.13) | data formatting | bytes 147456 | tf_op args[1]
  11.3 0.0 collective-permute-done
  11.4 0.0 copy-start.1
  11.4 2.8 %copy-done.1 = bf16[3,2048,512]{2,1,0:T(8,128)(2,1)S(1)} copy-done((bf16[3,2048,512]{2,1,0:T(8,128)(2,1)S(1)}, bf16[3,2048,512]{2,1,0:T(8,128)(2,1)}, u32[]{:S(2)}) %copy-start.1) | copy-done | bytes 6291480
  14.2 1.6 %copy-done.3 = f32[256,2048]{1,0:T(8,128)S(1)} copy-done((f32[256,2048]{1,0:T(8,128)S(1)}, f32[256,2048]{1,0:T(8,128)}, u32[]{:S(2)}) %copy-start.3) | copy-done | bytes 2097176
  15.8 0.0 copy-start.8
  15.8 0.0 copy-start.9
  15.8 0.0 copy-start.11
  15.8 14.9 %front.1 = (bf16[2048,512]{1,0:T(8,128)(2,1)S(1)}, f32[64,2048]{1,0:T(8,128)S(1)}, bf16[16,2048]{1,0:T(8,128)(2,1)S(1)}) custom-call(bf16[3,2048,512]{2,1,0:T(8,128)(2,1)S(1)} %copy-done.1, bf16[8,2048]{1,0:T(8,128)(2,1)S(1)} %pad.4.halo_ref, f32[3,2048,3]{2,1,0:T(8,128)S(1)} %copy.16.w_ref, f32[256,2048]{1,0:T(8,128)S(1)} %copy-done.3, ...), custom_call_target="tpu_custom_call" | custom-call | tf_op jit(solution)/shard_map/front/pallas_call | solution.py:180
  30.7 31.9 %all-gather = bf16[128,2048]{1,0:T(8,128)(2,1)S(1)} all-gather(bf16[16,2048]{1,0:T(8,128)(2,1)S(1)} %get-tuple-element.10), channel_id=2, replica_groups=mesh['seq'=8,'fsdp'=4] {'seq'}, dimensions={0}, use_global_device_ids=true | all-gather | bytes 589824 | tf_op jit(solution)/shard_map/all_gather | solution.py:194
  62.6 0.2 fusion
  62.8 0.0 copy-done.4
  62.8 14.6 %back.1 = bf16[2048,512]{1,0:T(8,128)(2,1)} custom-call(bf16[3,2048,512]{2,1,0:T(8,128)(2,1)} %q_ref.1, bf16[2048,512]{1,0:T(8,128)(2,1)S(1)} %get-tuple-element.8.mixed_ref, bf16[8,2048]{1,0:T(8,128)(2,1)S(1)} %pad.4.halo_ref, f32[3,2048,3]{2,1,0:T(8,128)S(1)} %copy.16.w_ref, f32[256,2048]{1,0:T(8,128)S(1)} %copy-done.4, f32[16,2048]{1,0:T(8,128)S(1)} %bitcast.87, ...), custom_call_target="tpu_custom_call" | custom-call | tf_op jit(solution)/shard_map/back/pallas_call | solution.py:199
  (23 shorter events, 0.2 us)
Async XLA Ops:
  0.0 7.7 %copy-start = (f32[2048,16]{0,1:T(8,128)S(1)}, f32[2048,16]{0,1:T(8,128)}, u32[]{:S(2)}) copy-start(f32[2048,16]{0,1:T(8,128)} %param.14) | copy-start | bytes 393220
  2.7 7.6 %copy-start.13 = (f32[3,2048,3]{1,2,0:T(4,128)S(1)}, f32[3,2048,3]{1,2,0:T(4,128)}, u32[]{:S(2)}) copy-start(f32[3,2048,3]{1,2,0:T(4,128)} %param.12) | copy-start | bytes 221188
  2.7 8.7 %collective-permute-start = (bf16[3,2,2048]{2,1,0:T(2,128)(2,1)S(1)}, bf16[3,2,2048]{2,1,0:T(2,128)(2,1)S(1)}, u32[]{:S(2)}, u32[]{:S(2)}) collective-permute-start(bf16[3,2,2048]{2,1,0:T(2,128)(2,1)S(1)} %bitcast.89), channel_id=1, source_target_pairs={{0,4},{4,8},{8,12},{12,16},{16,20},{20,24},{24,28},{1,5},{5,9},{9,... | collective-permute-start | bytes 73736 | tf_op jit(solution)/shard_map/ppermute | solution.py:163
  8.5 2.9 %copy-start.7 = (bf16[8,768]{1,0:T(8,128)(2,1)S(1)}, bf16[8,768]{1,0:T(8,128)(2,1)}, u32[]{:S(2)}) copy-start(bf16[8,768]{1,0:T(8,128)(2,1)} %constant.53.clone.sel_ref) | copy-start | bytes 36868
  8.5 2.9 %copy-start.10 = (bf16[64,256]{1,0:T(8,128)(2,1)S(1)}, bf16[64,256]{1,0:T(8,128)(2,1)}, u32[]{:S(2)}) copy-start(bf16[64,256]{1,0:T(8,128)(2,1)} %constant.51.clone.mom_ref) | copy-start | bytes 98308
  9.0 1.3 %copy-start.2 = (f32[256,2048]{1,0:T(8,128)}, f32[256,2048]{1,0:T(8,128)S(1)}, u32[]{:S(2)}) copy-start(f32[256,2048]{1,0:T(8,128)S(1)} %subtract_dynamic-update-slice_fusion.cheb_ref) | copy-start | bytes 6291460
  11.4 2.8 %copy-start.1 = (bf16[3,2048,512]{2,1,0:T(8,128)(2,1)S(1)}, bf16[3,2048,512]{2,1,0:T(8,128)(2,1)}, u32[]{:S(2)}) copy-start(bf16[3,2048,512]{2,1,0:T(8,128)(2,1)} %q_ref.1) | copy-start | bytes 18874372
  14.2 1.6 %copy-start.3 = (f32[256,2048]{1,0:T(8,128)S(1)}, f32[256,2048]{1,0:T(8,128)}, u32[]{:S(2)}) copy-start(f32[256,2048]{1,0:T(8,128)} %copy-done.2) | copy-start | bytes 6291460
  15.8 46.8 %copy-start.12 = (f32[2048,16]{0,1:T(8,128)S(1)}, f32[2048,16]{0,1:T(8,128)}, u32[]{:S(2)}) copy-start(f32[2048,16]{0,1:T(8,128)} %param.15) | copy-start | bytes 393220
  15.8 47.0 %copy-start.4 = (f32[256,2048]{1,0:T(8,128)S(1)}, f32[256,2048]{1,0:T(8,128)}, u32[]{:S(2)}) copy-start(f32[256,2048]{1,0:T(8,128)} %copy-done.2) | copy-start | bytes 6291460
  15.8 47.0 %copy-start.5 = (bf16[256,256]{1,0:T(8,128)(2,1)S(1)}, bf16[256,256]{1,0:T(8,128)(2,1)}, u32[]{:S(2)}) copy-start(bf16[256,256]{1,0:T(8,128)(2,1)} %constant.49.clone.inv_ref) | copy-start | bytes 393220
  15.8 47.0 %copy-start.6 = (bf16[256,256]{1,0:T(8,128)(2,1)S(1)}, bf16[256,256]{1,0:T(8,128)(2,1)}, u32[]{:S(2)}) copy-start(bf16[256,256]{1,0:T(8,128)(2,1)} %constant.48.clone.fwd_ref) | copy-start | bytes 393220
  15.8 47.0 %copy-start.8 = (bf16[96,256]{1,0:T(8,128)(2,1)S(1)}, bf16[96,256]{1,0:T(8,128)(2,1)}, u32[]{:S(2)}) copy-start(bf16[96,256]{1,0:T(8,128)(2,1)} %constant.52.clone.car_ref) | copy-start | bytes 147460
  15.8 47.0 %copy-start.9 = (bf16[96,256]{1,0:T(8,128)(2,1)S(1)}, bf16[96,256]{1,0:T(8,128)(2,1)}, u32[]{:S(2)}) copy-start(bf16[96,256]{1,0:T(8,128)(2,1)} %constant.50.clone.spec_ref) | copy-start | bytes 147460
  15.8 47.0 %copy-start.11 = (f32[2048]{0:T(1024)S(1)}, f32[2048]{0:T(1024)}, u32[]{:S(2)}) copy-start(f32[2048]{0:T(1024)} %param.13) | copy-start | bytes 24580

commit v2 on v1

v2 whole, which is shorter than its diff:
```python
import functools
import math

import jax
import jax.numpy as jnp
import numpy as np
from jax import lax
from jax.experimental import pallas as pl
from jax.experimental.pallas import tpu as pltpu
from jax.sharding import PartitionSpec as P

BL = 128
NB = 16
HALF = 0.025


def split(m):
    hi = m.astype(jnp.bfloat16)
    return hi, (m - np.asarray(hi, np.float64)).astype(jnp.bfloat16)


@functools.cache
def tables():
    nodes = 64
    theta = (np.arange(nodes) + 0.5) * np.pi / nodes
    t = np.arange(BL + 1)
    f = np.exp(-HALF * (1 + np.cos(theta))[:, None] * t[None, :])
    psi = np.stack(
        [(2.0 if n else 1.0) / nodes * (np.cos(n * theta) @ f) for n in range(NB)]
    )
    half = BL // 2
    ang = np.pi * np.outer(np.arange(BL), 2 * np.arange(half) + 1) / BL
    c, s = np.cos(ang), np.sin(ang)
    z = np.zeros_like(c)
    fwd = np.block([[c, z, -s, z], [z, c, z, -s]])
    inv = np.block([[c, z, -s, z], [z, c, z, -s]]).T * (2.0 / BL)
    spec = np.concatenate([psi[:, :BL] @ c] * 2 + [-psi[:, :BL] @ s] * 2, axis=1)
    unit = np.concatenate([np.ones((1, BL)), np.zeros((1, BL))], axis=1)
    spec = np.concatenate([spec, unit, np.zeros((15, 2 * BL))], axis=0)
    rev = psi[:, BL - 1 :: -1][:, :BL]
    zr = np.zeros_like(rev)
    mom = np.block([[rev, zr], [zr, rev]])
    nxt = psi[:, 1 : BL + 1]
    car = np.block([[nxt, zr], [zr, nxt]])
    sh, sl = split(spec)
    mh, ml = split(mom)
    ch, cl = split(car)
    sel = np.zeros((8, 6 * 128))
    for i in range(3):
        sel[2 * i + 1, (2 * i) * 128] = 1
        sel[2 * i, (2 * i + 1) * 128] = 1
        sel[2 * i + 1, (2 * i + 1) * 128 + 1] = 1
    wide = np.kron(np.eye(9), np.ones((1, 128)))
    wide = np.concatenate([wide, np.zeros((7, 9 * 128))], axis=0)
    wide = np.concatenate([wide, wide], axis=0)
    cat = lambda *a: np.concatenate(a, axis=0)
    b16 = lambda a: a.astype(jnp.bfloat16)
    return dict(
        fwd=b16(fwd), inv=b16(inv), spec=cat(sh, sh, sl), mom=cat(mh, ml),
        car=cat(ch, ch, cl), sel=b16(sel), wide=b16(wide),
    )


def rowdot(a, b):
    return lax.dot_general(a, b, (((0,), (0,)), ((), ())), preferred_element_type=jnp.float32)


def three(m):
    hi = m.astype(jnp.bfloat16)
    lo = (m - hi.astype(jnp.float32)).astype(jnp.bfloat16)
    return jnp.concatenate([hi, lo, hi], axis=0)


def dot(a, b):
    return jnp.dot(a, b, preferred_element_type=jnp.float32)


def two(m):
    hi = m.astype(jnp.bfloat16)
    lo = (m - hi.astype(jnp.float32)).astype(jnp.bfloat16)
    return jnp.concatenate([hi, lo], axis=0)


def series(decay, cheb_ref):
    xi = decay * (1.0 / HALF) - 1.0
    a, b = jnp.ones_like(xi), xi
    for n in range(NB):
        cheb_ref[n * 16 : n * 16 + 16] = a
        a, b = b, 2.0 * xi * b - a


def feat(x, w_ref, rows, h1, h2, first):
    lane = lax.broadcasted_iota(jnp.int32, (x.shape[0], 128), 1)
    w0, w1, w2 = (w_ref[rows, (first + i) * 128 : (first + i + 1) * 128] for i in range(3))
    out = []
    for i in range(x.shape[1] // 128):
        c = x[:, i * 128 : (i + 1) * 128].astype(jnp.float32)
        r1, r2 = pltpu.roll(c, 1, 1), pltpu.roll(c, 2, 1)
        out.append(w0 * c + w1 * jnp.where(lane < 1, h1, r1) + w2 * jnp.where(lane < 2, h2, r2))
        h1, h2 = r1, r2
    return out


ROWS = 64


def front(p_ref, halo_ref, w_ref, decay_ref, sel_ref, wide_ref, mom_ref,
          mixed_ref, ends_ref, last_ref, power_ref,
          hr_ref, wide_w, cheb_ref):
    tile, length = p_ref.shape[1:]
    hr_ref[...] = rowdot(halo_ref[...], sel_ref[:, 256:])
    wide_w[...] = rowdot(two(w_ref[...]), wide_ref[:, 384:])
    series(decay_ref[...], cheb_ref)

    @pl.loop(0, tile // ROWS)
    def _(r):
        rows = pl.ds(pl.multiple_of(r * ROWS, ROWS), ROWS)
        k = feat(p_ref[0, rows, :], wide_w, rows, hr_ref[rows, 0:128], hr_ref[rows, 128:256], 0)
        v = feat(p_ref[1, rows, :], wide_w, rows, hr_ref[rows, 256:384], hr_ref[rows, 384:512], 3)
        for i in range(len(k)):
            mixed_ref[rows, i * 128 : (i + 1) * 128] = (k[i] * v[i]).astype(jnp.bfloat16)

    step = jnp.exp(-BL * decay_ref[...])
    total = None
    for pair in range(length // 256):
        m = lax.dot_general(
            mom_ref[...], mixed_ref[:, pair * 256 : (pair + 1) * 256],
            (((1,), (1,)), ((), ())), preferred_element_type=jnp.float32)
        m = m[:32] + m[32:]
        for b in range(2):
            e = cheb_ref[0:16] * m[b * 16 : b * 16 + 1]
            for i in range(1, NB):
                e = e + cheb_ref[i * 16 : i * 16 + 16] * m[b * 16 + i : b * 16 + i + 1]
            ends_ref[(pair * 2 + b) * 16 : (pair * 2 + b + 1) * 16] = e
            total = e if total is None else step * total + e
    last_ref[...] = total.astype(last_ref.dtype)
    power_ref[...] = jnp.exp(-length * decay_ref[...])


def exchange(n, last_ref, power_ref, init_ref, inbox, send_sem, recv_sem):
    me = lax.axis_index("seq")
    barrier = pltpu.get_barrier_semaphore()

    @pl.loop(0, n)
    def _(j):
        @pl.when(j != me)
        def _():
            pl.semaphore_signal(barrier, inc=1, device_id={"seq": j}, device_id_type=pl.DeviceIdType.MESH)

    pl.semaphore_wait(barrier, n - 1)

    def copy(j, source):
        return pltpu.make_async_remote_copy(
            src_ref=last_ref, dst_ref=inbox.at[source],
            send_sem=send_sem.at[j], recv_sem=recv_sem.at[source],
            device_id={"seq": j}, device_id_type=pl.DeviceIdType.MESH)

    @pl.loop(0, n)
    def _(j):
        @pl.when(j > me)
        def _():
            copy(j, me).start()

    init_ref[...] = jnp.zeros_like(init_ref)

    @pl.loop(0, n)
    def _(j):
        @pl.when(j < me)
        def _():
            copy(me, j).wait_recv()
            init_ref[...] = power_ref[...] * init_ref[...] + inbox[j].astype(jnp.float32)

    @pl.loop(0, n)
    def _(j):
        @pl.when(j > me)
        def _():
            copy(j, me).wait_send()


def back(q_ref, mixed_ref, halo_ref, w_ref, decay_ref, residue_ref, skip_ref, ends_ref, init_ref,
         sel_ref, wide_ref, fwd_ref, inv_ref, spec_ref, car_ref,
         out_ref, hr_ref, h_ref, y_ref, wide_w, cheb_ref):
    tile = mixed_ref.shape[0]
    hr_ref[...] = rowdot(halo_ref[...], sel_ref[:, :256])
    wide_w[...] = rowdot(two(w_ref[...]), wide_ref[:, :384])
    series(decay_ref[...], cheb_ref)
    step = jnp.exp(-BL * decay_ref[...])
    fold = 1.0 / (1.0 + step)
    weight = residue_ref[...] * jnp.sqrt(2.0 * decay_ref[...])
    wv = weight * fold
    g = [jnp.sum(wv * cheb_ref[n * 16 : n * 16 + 16], axis=0, keepdims=True) for n in range(NB)]
    g = jnp.concatenate(g + [skip_ref[...], jnp.zeros((15, tile), jnp.float32)], axis=0)
    h_ref[...] = rowdot(three(g), spec_ref[...])
    state = init_ref[...]
    for pair in range(mixed_ref.shape[1] // 256):
        c = []
        for b in range(2):
            e = ends_ref[(pair * 2 + b) * 16 : (pair * 2 + b + 1) * 16]
            p = weight * (state + fold * e)
            state = step * state + e
            c += [jnp.sum(p * cheb_ref[n * 16 : n * 16 + 16], axis=0, keepdims=True) for n in range(NB)]
        cols = slice(pair * 256, pair * 256 + 256)
        carried = rowdot(three(jnp.concatenate(c, axis=0)), car_ref[...])
        x = dot(mixed_ref[:, cols], fwd_ref[...])
        xr, xi = x[:, :128], x[:, 128:]
        hr, hi = h_ref[:, :128], h_ref[:, 128:]
        y = jnp.concatenate([xr * hr - xi * hi, xr * hi + xi * hr], axis=1).astype(jnp.bfloat16)
        y_ref[:, cols] = (carried + dot(y, inv_ref[...])).astype(jnp.bfloat16)

    @pl.loop(0, tile // ROWS)
    def _(r):
        rows = pl.ds(pl.multiple_of(r * ROWS, ROWS), ROWS)
        q = feat(q_ref[0, rows, :], wide_w, rows, hr_ref[rows, 0:128], hr_ref[rows, 128:256], 0)
        for i in range(len(q)):
            cols = slice(i * 128, i * 128 + 128)
            out_ref[rows, cols] = (q[i] * y_ref[rows, cols].astype(jnp.float32)).astype(jnp.bfloat16)


def shards(projected, short_weight, skip_weight, decay_rates, residues):
    channels, length = projected.shape[1:]
    n = lax.axis_size("seq")
    tab = {k: jnp.asarray(v) for k, v in tables().items()}
    tile = math.gcd(512, channels)
    blocks = length // BL
    tail = jnp.swapaxes(projected[:, :, length - 2 :], 1, 2)
    halo = lax.ppermute(tail, "seq", [(i, i + 1) for i in range(n - 1)])
    halo = jnp.pad(halo.reshape(6, channels), ((0, 2), (0, 0)))
    taps = jnp.swapaxes(short_weight, 1, 2).reshape(9, channels)
    taps = jnp.pad(taps, ((0, 7), (0, 0)))
    decay, residue = decay_rates.T, residues.T

    full = lambda a: pl.BlockSpec(a.shape, lambda i: (0,) * a.ndim)
    lanes = lambda r: pl.BlockSpec((r, tile), lambda i: (0, i))
    rows = pl.BlockSpec((tile, length), lambda i: (i, 0))
    limit = 56 * 2**20
    count = channels // tile
    names = ("sel", "wide", "mom")
    mixed, ends, last, power = pl.pallas_call(
        front,
        grid=(count,),
        in_specs=[pl.BlockSpec((pl.Element(2), pl.Element(tile), pl.Element(length)), lambda i: (1, i * tile, 0)),
                  lanes(8), lanes(16), lanes(16)] + [full(tab[k]) for k in names],
        out_specs=[rows, lanes(blocks * 16), lanes(16), lanes(16)],
        out_shape=[
            jax.ShapeDtypeStruct((channels, length), jnp.bfloat16),
            jax.ShapeDtypeStruct((blocks * 16, channels), jnp.float32),
            jax.ShapeDtypeStruct((16, channels), jnp.bfloat16),
            jax.ShapeDtypeStruct((16, channels), jnp.float32),
        ],
        scratch_shapes=[
            pltpu.VMEM((tile, 512), jnp.float32),
            pltpu.VMEM((tile, 6 * 128), jnp.float32),
            pltpu.VMEM((NB * 16, tile), jnp.float32),
        ],
        compiler_params=pltpu.CompilerParams(vmem_limit_bytes=limit),
        name="front",
    )(projected, halo, taps, decay, *[tab[k] for k in names])
    init = pl.pallas_call(
        functools.partial(exchange, n),
        in_specs=[pl.BlockSpec(memory_space=pltpu.VMEM)] * 2,
        out_specs=pl.BlockSpec(memory_space=pltpu.VMEM),
        out_shape=jax.ShapeDtypeStruct((16, channels), jnp.float32),
        scratch_shapes=[
            pltpu.VMEM((n, 16, channels), jnp.bfloat16),
            pltpu.SemaphoreType.DMA((n,)),
            pltpu.SemaphoreType.DMA((n,)),
        ],
        compiler_params=pltpu.CompilerParams(collective_id=0, has_side_effects=True),
        name="exchange",
    )(last, power)
    names = ("sel", "wide", "fwd", "inv", "spec", "car")
    return pl.pallas_call(
        back,
        grid=(count,),
        in_specs=[pl.BlockSpec((1, tile, length), lambda i: (0, i, 0)), rows, lanes(8), lanes(16), lanes(16),
                  lanes(16), lanes(1), lanes(blocks * 16), lanes(16)] + [full(tab[k]) for k in names],
        out_specs=rows,
        out_shape=jax.ShapeDtypeStruct((channels, length), jnp.bfloat16),
        scratch_shapes=[
            pltpu.VMEM((tile, 256), jnp.float32),
            pltpu.VMEM((tile, 256), jnp.float32),
            pltpu.VMEM((tile, length), jnp.bfloat16),
            pltpu.VMEM((tile, 3 * 128), jnp.float32),
            pltpu.VMEM((NB * 16, tile), jnp.float32),
        ],
        compiler_params=pltpu.CompilerParams(vmem_limit_bytes=limit),
        name="back",
    )(projected, mixed, halo, taps, decay, residue, skip_weight[None], ends, init, *[tab[k] for k in names])


def solution(mesh):
    return jax.shard_map(
        shards,
        mesh=mesh,
        in_specs=(
            P(None, "fsdp", "seq"),
            P(None, "fsdp", None),
            P("fsdp"),
            P("fsdp", None),
            P("fsdp", None),
        ),
        out_specs=P("fsdp", "seq"),
        check_vma=False,
    )
```

time: 77.7 us -> 48.4 us (0.62)
  the two profiles are of different devices: /device:TPU:0 before, /device:TPU:28 now
where the time goes in v2:
time: 48.4 us; the launch traced here: 48.2 us
  Pallas kernels  38.3 us (79%)
  local copies, waits for them, and re-layouts  3.99 us (8%)
  starting transfers between devices  3.4 us (7%)
  waiting for transfers between devices  2.49 us (5%)
    pallas_call x1, Pallas kernels, shards(): pl.pallas_call(functools.partial(exchange, n), in_specs=[pl.BlockSpec(mem...  15.5 us
    pallas_call x1, Pallas kernels, shards(): pl.pallas_call(front, grid=(count,), in_specs=[pl.BlockSpec((pl.Element(2...  11.4 us
    pallas_call x1, Pallas kernels, shards(): pl.pallas_call(back, grid=(count,), in_specs=[pl.BlockSpec((1, tile, leng...  11.4 us
    ppermute x1, starting transfers between devices, shards(): halo = lax.ppermute(tail, 'seq', [(i, i + 1) for i in range(n - 1)])  3.4 us
    ppermute x1, waiting for transfers between devices, shards(): halo = lax.ppermute(tail, 'seq', [(i, i + 1) for i in range(n - 1)])  2.49 us
    slice x1, local copies, waits for them, and re-layouts, shards(): tail = jnp.swapaxes(projected[:, :, length - 2:], 1, 2)  1.93 us
  transfers between devices with their start and end apart: 1, of which 1 were waited for; matrix products, arithmetic and copies ran while one was open for 1% of the time, Pallas kernels for 0%

profile of v2, /device:TPU:28, one launch (start us, length us, event | category | flops | bytes accessed | tf_op | source)
XLA Modules:
  0.0 48.2 jit_solution(14830782152366933856)
XLA Ops:
  0.0 0.0 copy-start
  0.0 1.9 %slice.3 = bf16[3,2048,2]{2,1,0:T(8,128)(2,1)S(1)} slice(bf16[3,2048,512]{2,1,0:T(8,128)(2,1)} %q_ref.1), slice={[0:3], [0:2048], [510:512]} | slice | bytes 49152 | tf_op jit(solution)/shard_map/slice | solution.py:225
  1.9 0.7 %copy.15 = bf16[3,2048,2]{1,2,0:T(2,128)(2,1)S(1)} copy(bf16[3,2048,2]{2,1,0:T(8,128)(2,1)S(1)} %slice.3) | data formatting | bytes 49152
  2.7 3.4 %collective-permute-start = (bf16[3,2,2048]{2,1,0:T(2,128)(2,1)S(1)}, bf16[3,2,2048]{2,1,0:T(2,128)(2,1)S(1)}, u32[]{:S(2)}, u32[]{:S(2)}) collective-permute-start(bf16[3,2,2048]{2,1,0:T(2,128)(2,1)S(1)} %bitcast.9), channel_id=1, source_target_pairs={{0,4},{4,8},{8,12},{12,16},{16,20},{20,24},{24,28},{1,5},{5,9},{9,... | collective-permute-start | bytes 73736 | tf_op jit(solution)/shard_map/ppermute | solution.py:226
  6.1 0.0 copy-done
  6.1 0.7 %pad.9.w_ref = f32[16,2048]{1,0:T(8,128)} pad(f32[9,2048]{1,0:T(8,128)S(1)} %reshape.7, f32[]{:T(128)} %constant.18.clone.1), padding=0_7x0_0 | pad | bytes 204804 | tf_op jit(solution)/shard_map/jit(_pad)/pad | solution.py:229
  6.8 2.5 %collective-permute-done = bf16[3,2,2048]{2,1,0:T(2,128)(2,1)S(1)} collective-permute-done((bf16[3,2,2048]{2,1,0:T(2,128)(2,1)S(1)}, bf16[3,2,2048]{2,1,0:T(2,128)(2,1)S(1)}, u32[]{:S(2)}, u32[]{:S(2)}) %collective-permute-start) | collective-permute-done | bytes 24608 | tf_op jit(solution)/shard_map/ppermute | solution.py:226
  9.3 0.6 %pad.8.halo_ref = bf16[8,2048]{1,0:T(8,128)(2,1)} pad(bf16[6,2048]{1,0:T(8,128)(2,1)S(1)} %reshape.6, bf16[]{:T(256)} %constant.17.clone.1), padding=0_2x0_0 | pad | bytes 57346 | tf_op jit(solution)/shard_map/jit(_pad)/pad | solution.py:227
  9.9 11.4 %front.1 = (bf16[2048,512]{1,0:T(8,128)(2,1)}, f32[64,2048]{1,0:T(8,128)}, bf16[16,2048]{1,0:T(8,128)(2,1)}, f32[16,2048]{1,0:T(8,128)}) custom-call(bf16[3,2048,512]{2,1,0:T(8,128)(2,1)} %q_ref.1, bf16[8,2048]{1,0:T(8,128)(2,1)} %pad.8.halo_ref, f32[16,2048]{1,0:T(8,128)} %pad.9.w_ref, f32[16,2048]{1,0:T(8,128)} %bitcast.5, ...), custom_call_target="tpu_custom_call" | custom-call | tf_op jit(solution)/shard_map/front/pallas_call | solution.py:238
  21.3 15.5 %exchange.1.init_ref = f32[16,2048]{1,0:T(8,128)} custom-call(bf16[16,2048]{1,0:T(8,128)(2,1)} %get-tuple-element.11.last_ref, f32[16,2048]{1,0:T(8,128)} %get-tuple-element.12.power_ref), custom_call_target="tpu_custom_call" | custom-call | tf_op jit(solution)/shard_map/exchange/pallas_call | solution.py:258
  36.9 11.4 %back.1 = bf16[2048,512]{1,0:T(8,128)(2,1)} custom-call(bf16[3,2048,512]{2,1,0:T(8,128)(2,1)} %q_ref.1, bf16[2048,512]{1,0:T(8,128)(2,1)} %get-tuple-element.9.mixed_ref, bf16[8,2048]{1,0:T(8,128)(2,1)} %pad.8.halo_ref, f32[16,2048]{1,0:T(8,128)} %pad.9.w_ref, f32[16,2048]{1,0:T(8,128)} %bitcast.6, f32[16,2048]{1,0:T(8,128)} %bitcast.7, f32[1,2048]{1,0:T(1,128)} %bitcast.10, ...), custom_call_target="tpu_custom_call" | custom-call | tf_op jit(solution)/shard_map/back/pallas_call | solution.py:272
  (2 shorter events, 0.1 us)
Async XLA Ops:
  0.0 6.1 %copy-start = (f32[3,2048,3]{1,2,0:T(4,128)S(1)}, f32[3,2048,3]{1,2,0:T(4,128)}, u32[]{:S(2)}) copy-start(f32[3,2048,3]{1,2,0:T(4,128)} %param.13) | copy-start | bytes 221188
  2.7 6.6 %collective-permute-start = (bf16[3,2,2048]{2,1,0:T(2,128)(2,1)S(1)}, bf16[3,2,2048]{2,1,0:T(2,128)(2,1)S(1)}, u32[]{:S(2)}, u32[]{:S(2)}) collective-permute-start(bf16[3,2,2048]{2,1,0:T(2,128)(2,1)S(1)} %bitcast.9), channel_id=1, source_target_pairs={{0,4},{4,8},{8,12},{12,16},{16,20},{20,24},{24,28},{1,5},{5,9},{9,... | collective-permute-start | bytes 73736 | tf_op jit(solution)/shard_map/ppermute | solution.py:226

commit v3 on v2

--- a/solution.py
+++ b/solution.py
@@ -81,6 +81,11 @@
     return jnp.concatenate([hi, lo], axis=0)
 
 
+def padded(m, count):
+    m = m.astype(jnp.float32)
+    return jnp.concatenate([m, jnp.zeros((count - m.shape[0], m.shape[1]), jnp.float32)], axis=0)
+
+
 def series(decay, cheb_ref):
     xi = decay * (1.0 / HALF) - 1.0
     a, b = jnp.ones_like(xi), xi
@@ -108,8 +113,8 @@
           mixed_ref, ends_ref, last_ref, power_ref,
           hr_ref, wide_w, cheb_ref):
     tile, length = p_ref.shape[1:]
-    hr_ref[...] = rowdot(halo_ref[...], sel_ref[:, 256:])
-    wide_w[...] = rowdot(two(w_ref[...]), wide_ref[:, 384:])
+    hr_ref[...] = rowdot(padded(halo_ref[...], 8).astype(jnp.bfloat16), sel_ref[:, 256:])
+    wide_w[...] = rowdot(two(padded(w_ref[...], 16)), wide_ref[:, 384:])
     series(decay_ref[...], cheb_ref)
 
     @pl.loop(0, tile // ROWS)
@@ -137,52 +142,89 @@
     power_ref[...] = jnp.exp(-length * decay_ref[...])
 
 
-def exchange(n, last_ref, power_ref, init_ref, inbox, send_sem, recv_sem):
+def exchange(n, last_ref, power_ref, init_ref, peer, pair, inbox, give, got, send_sem, recv_sem, swap_send, swap_recv):
     me = lax.axis_index("seq")
+    odd = lax.rem(me, 2)
+    partner = me + 1 - 2 * odd
+    half = last_ref.shape[1] // 2
+    own = pl.ds(pl.multiple_of(odd * half, half), half)
+    other = pl.ds(pl.multiple_of((1 - odd) * half, half), half)
     barrier = pltpu.get_barrier_semaphore()
 
-    @pl.loop(0, n)
-    def _(j):
-        @pl.when(j != me)
+    def greet(j):
+        pl.semaphore_signal(barrier, inc=1, device_id={"seq": j}, device_id_type=pl.DeviceIdType.MESH)
+
+    greet(partner)
+
+    @pl.loop(0, n // 2)
+    def _(i):
+        @pl.when(2 * i + odd != me)
         def _():
-            pl.semaphore_signal(barrier, inc=1, device_id={"seq": j}, device_id_type=pl.DeviceIdType.MESH)
-
-    pl.semaphore_wait(barrier, n - 1)
-
-    def copy(j, source):
+            greet(2 * i + odd)
+
+    pl.semaphore_wait(barrier, n // 2)
+
+    def swap(src, dst, i):
         return pltpu.make_async_remote_copy(
-            src_ref=last_ref, dst_ref=inbox.at[source],
-            send_sem=send_sem.at[j], recv_sem=recv_sem.at[source],
-            device_id={"seq": j}, device_id_type=pl.DeviceIdType.MESH)
-
-    @pl.loop(0, n)
-    def _(j):
-        @pl.when(j > me)
+            src_ref=src, dst_ref=dst, send_sem=swap_send.at[i], recv_sem=swap_recv.at[i],
+            device_id={"seq": partner}, device_id_type=pl.DeviceIdType.MESH)
+
+    def copy(i, source):
+        return pltpu.make_async_remote_copy(
+            src_ref=pair, dst_ref=inbox.at[source], send_sem=send_sem.at[i], recv_sem=recv_sem.at[source],
+            device_id={"seq": 2 * i + odd}, device_id_type=pl.DeviceIdType.MESH)
+
+    at = lax.div(me, 2)
+    first = swap(last_ref.at[:, other], peer, 0)
+    first.start()
+    power = power_ref[:, own]
+    mine = last_ref[:, own].astype(jnp.float32)
+    first.wait_recv()
+    theirs = peer[...].astype(jnp.float32)
+    even = odd == 0
+    e0 = jnp.where(even, mine, theirs)
+    e1 = jnp.where(even, theirs, mine)
+    pair[...] = (power * e0 + e1).astype(pair.dtype)
+
+    @pl.loop(0, n // 2)
+    def _(i):
+        @pl.when(i > at)
         def _():
-            copy(j, me).start()
-
-    init_ref[...] = jnp.zeros_like(init_ref)
-
-    @pl.loop(0, n)
-    def _(j):
-        @pl.when(j < me)
+            copy(i, at).start()
+
+    init_ref[:, own] = jnp.zeros((16, half), jnp.float32)
+
+    @pl.loop(0, n // 2)
+    def _(i):
+        @pl.when(i < at)
         def _():
-            copy(me, j).wait_recv()
-            init_ref[...] = power_ref[...] * init_ref[...] + inbox[j].astype(jnp.float32)
-
-    @pl.loop(0, n)
-    def _(j):
-        @pl.when(j > me)
+            copy(at, i).wait_recv()
+            init_ref[:, own] = power * power * init_ref[:, own] + inbox[i].astype(jnp.float32)
+
+    start = init_ref[:, own]
+    later = power * start + e0
+    give[...] = jnp.where(even, later, start).astype(give.dtype)
+    second = swap(give, got, 1)
+    second.start()
+    init_ref[:, own] = jnp.where(even, start, later)
+    second.wait_recv()
+    init_ref[:, other] = got[...].astype(jnp.float32)
+    first.wait_send()
+    second.wait_send()
+
+    @pl.loop(0, n // 2)
+    def _(i):
+        @pl.when(i > at)
         def _():
-            copy(j, me).wait_send()
+            copy(i, at).wait_send()
 
 
 def back(q_ref, mixed_ref, halo_ref, w_ref, decay_ref, residue_ref, skip_ref, ends_ref, init_ref,
          sel_ref, wide_ref, fwd_ref, inv_ref, spec_ref, car_ref,
          out_ref, hr_ref, h_ref, y_ref, wide_w, cheb_ref):
     tile = mixed_ref.shape[0]
-    hr_ref[...] = rowdot(halo_ref[...], sel_ref[:, :256])
-    wide_w[...] = rowdot(two(w_ref[...]), wide_ref[:, :384])
+    hr_ref[...] = rowdot(padded(halo_ref[...], 8).astype(jnp.bfloat16), sel_ref[:, :256])
+    wide_w[...] = rowdot(two(padded(w_ref[...], 16)), wide_ref[:, :384])
     series(decay_ref[...], cheb_ref)
     step = jnp.exp(-BL * decay_ref[...])
     fold = 1.0 / (1.0 + step)
@@ -224,9 +266,8 @@
     blocks = length // BL
     tail = jnp.swapaxes(projected[:, :, length - 2 :], 1, 2)
     halo = lax.ppermute(tail, "seq", [(i, i + 1) for i in range(n - 1)])
-    halo = jnp.pad(halo.reshape(6, channels), ((0, 2), (0, 0)))
+    halo = halo.reshape(6, channels)
     taps = jnp.swapaxes(short_weight, 1, 2).reshape(9, channels)
-    taps = jnp.pad(taps, ((0, 7), (0, 0)))
     decay, residue = decay_rates.T, residues.T
 
     full = lambda a: pl.BlockSpec(a.shape, lambda i: (0,) * a.ndim)
@@ -239,7 +280,7 @@
         front,
         grid=(count,),
         in_specs=[pl.BlockSpec((pl.Element(2), pl.Element(tile), pl.Element(length)), lambda i: (1, i * tile, 0)),
-                  lanes(8), lanes(16), lanes(16)] + [full(tab[k]) for k in names],
+                  lanes(6), lanes(9), lanes(16)] + [full(tab[k]) for k in names],
         out_specs=[rows, lanes(blocks * 16), lanes(16), lanes(16)],
         out_shape=[
             jax.ShapeDtypeStruct((channels, length), jnp.bfloat16),
@@ -261,9 +302,15 @@
         out_specs=pl.BlockSpec(memory_space=pltpu.VMEM),
         out_shape=jax.ShapeDtypeStruct((16, channels), jnp.float32),
         scratch_shapes=[
-            pltpu.VMEM((n, 16, channels), jnp.bfloat16),
-            pltpu.SemaphoreType.DMA((n,)),
-            pltpu.SemaphoreType.DMA((n,)),
+            pltpu.VMEM((16, channels // 2), jnp.bfloat16),
+            pltpu.VMEM((16, channels // 2), jnp.bfloat16),
+            pltpu.VMEM((n // 2, 16, channels // 2), jnp.bfloat16),
+            pltpu.VMEM((16, channels // 2), jnp.bfloat16),
+            pltpu.VMEM((16, channels // 2), jnp.bfloat16),
+            pltpu.SemaphoreType.DMA((n // 2,)),
+            pltpu.SemaphoreType.DMA((n // 2,)),
+            pltpu.SemaphoreType.DMA((2,)),
+            pltpu.SemaphoreType.DMA((2,)),
         ],
         compiler_params=pltpu.CompilerParams(collective_id=0, has_side_effects=True),
         name="exchange",
@@ -272,7 +319,7 @@
     return pl.pallas_call(
         back,
         grid=(count,),
-        in_specs=[pl.BlockSpec((1, tile, length), lambda i: (0, i, 0)), rows, lanes(8), lanes(16), lanes(16),
+        in_specs=[pl.BlockSpec((1, tile, length), lambda i: (0, i, 0)), rows, lanes(6), lanes(9), lanes(16),
                   lanes(16), lanes(1), lanes(blocks * 16), lanes(16)] + [full(tab[k]) for k in names],
         out_specs=rows,
         out_shape=jax.ShapeDtypeStruct((channels, length), jnp.bfloat16),

time: 48.4 us -> 47 us (0.971)
  Pallas kernels: 38.3 us -> 36.9 us
    pallas_call x1, Pallas kernels: 15.5 us -> 14 us  [shards(): pl.pallas_call(functools.partial(exchange, n), in_specs=[pl.BlockSpec(mem...]
    pad x2 -> x0, local copies, waits for them, and re-layouts: 1.28 us -> none  [the longest x1 0.67 us: shards(): taps = jnp.pad(taps, ((0, 7), (0, 0)))]
    reshape x1, local copies, waits for them, and re-layouts: 0.04 us -> 0.69 us  [shards(): taps = jnp.swapaxes(short_weight, 1, 2).reshape(9, channels)]
    reshape x1, local copies, waits for them, and re-layouts: 0.02 us -> 0.62 us  [shards(): halo = halo.reshape(6, channels)]
where the time goes in v3:
time: 47 us; the launch traced here: 46.8 us
  Pallas kernels  36.9 us (79%)
  local copies, waits for them, and re-layouts  3.96 us (8%)
  starting transfers between devices  3.4 us (7%)
  waiting for transfers between devices  2.51 us (5%)
    pallas_call x1, Pallas kernels, shards(): pl.pallas_call(functools.partial(exchange, n), in_specs=[pl.BlockSpec(mem...  14 us
    pallas_call x1, Pallas kernels, shards(): pl.pallas_call(front, grid=(count,), in_specs=[pl.BlockSpec((pl.Element(2...  11.4 us
    pallas_call x1, Pallas kernels, shards(): pl.pallas_call(back, grid=(count,), in_specs=[pl.BlockSpec((1, tile, leng...  11.4 us
    ppermute x1, starting transfers between devices, shards(): halo = lax.ppermute(tail, 'seq', [(i, i + 1) for i in range(n - 1)])  3.4 us
    ppermute x1, waiting for transfers between devices, shards(): halo = lax.ppermute(tail, 'seq', [(i, i + 1) for i in range(n - 1)])  2.51 us
    slice x1, local copies, waits for them, and re-layouts, shards(): tail = jnp.swapaxes(projected[:, :, length - 2:], 1, 2)  1.93 us
  transfers between devices with their start and end apart: 1, of which 1 were waited for; matrix products, arithmetic and copies ran while one was open for 1% of the time, Pallas kernels for 0%

profile of v3, /device:TPU:28, one launch (start us, length us, event | category | flops | bytes accessed | tf_op | source)
XLA Modules:
  0.0 46.8 jit_solution(3172236069328120437)
XLA Ops:
  0.0 0.0 copy-start
  0.0 1.9 %slice.3 = bf16[3,2048,2]{2,1,0:T(8,128)(2,1)S(1)} slice(bf16[3,2048,512]{2,1,0:T(8,128)(2,1)} %q_ref.1), slice={[0:3], [0:2048], [510:512]} | slice | bytes 49152 | tf_op jit(solution)/shard_map/slice | solution.py:267
  1.9 0.7 %copy.15 = bf16[3,2048,2]{1,2,0:T(2,128)(2,1)S(1)} copy(bf16[3,2048,2]{2,1,0:T(8,128)(2,1)S(1)} %slice.3) | data formatting | bytes 49152
  2.7 3.4 %collective-permute-start = (bf16[3,2,2048]{2,1,0:T(2,128)(2,1)S(1)}, bf16[3,2,2048]{2,1,0:T(2,128)(2,1)S(1)}, u32[]{:S(2)}, u32[]{:S(2)}) collective-permute-start(bf16[3,2,2048]{2,1,0:T(2,128)(2,1)S(1)} %bitcast.9), channel_id=1, source_target_pairs={{0,4},{4,8},{8,12},{12,16},{16,20},{20,24},{24,28},{1,5},{5,9},{9,... | collective-permute-start | bytes 73736 | tf_op jit(solution)/shard_map/ppermute | solution.py:268
  6.1 0.0 copy-done
  6.1 0.7 %reshape.7.w_ref = f32[9,2048]{1,0:T(8,128)} reshape(f32[3,3,2048]{2,1,0:T(4,128)S(1)} %bitcast.8) | data formatting | bytes 147456 | tf_op jit(solution)/shard_map/reshape | solution.py:270
  6.8 2.5 %collective-permute-done = bf16[3,2,2048]{2,1,0:T(2,128)(2,1)S(1)} collective-permute-done((bf16[3,2,2048]{2,1,0:T(2,128)(2,1)S(1)}, bf16[3,2,2048]{2,1,0:T(2,128)(2,1)S(1)}, u32[]{:S(2)}, u32[]{:S(2)}) %collective-permute-start) | collective-permute-done | bytes 24608 | tf_op jit(solution)/shard_map/ppermute | solution.py:268
  9.3 0.6 %reshape.6.halo_ref = bf16[6,2048]{1,0:T(8,128)(2,1)} reshape(bf16[3,2,2048]{2,1,0:T(2,128)(2,1)S(1)} %collective-permute-done) | data formatting | bytes 49152 | tf_op jit(solution)/shard_map/reshape | solution.py:269
  9.9 11.4 %front.1 = (bf16[2048,512]{1,0:T(8,128)(2,1)}, f32[64,2048]{1,0:T(8,128)}, bf16[16,2048]{1,0:T(8,128)(2,1)}, f32[16,2048]{1,0:T(8,128)}) custom-call(bf16[3,2048,512]{2,1,0:T(8,128)(2,1)} %q_ref.1, bf16[6,2048]{1,0:T(8,128)(2,1)} %reshape.6.halo_ref, f32[9,2048]{1,0:T(8,128)} %reshape.7.w_ref, f32[16,2048]{1,0:T(8,128)} %bitcast.5, ...), custom_call_target="tpu_custom_call" | custom-call | tf_op jit(solution)/shard_map/front/pallas_call | solution.py:279
  21.3 14.0 %exchange.1.init_ref = f32[16,2048]{1,0:T(8,128)} custom-call(bf16[16,2048]{1,0:T(8,128)(2,1)} %get-tuple-element.11.last_ref, f32[16,2048]{1,0:T(8,128)} %get-tuple-element.12.power_ref), custom_call_target="tpu_custom_call" | custom-call | tf_op jit(solution)/shard_map/exchange/pallas_call | solution.py:299
  35.4 11.4 %back.1 = bf16[2048,512]{1,0:T(8,128)(2,1)} custom-call(bf16[3,2048,512]{2,1,0:T(8,128)(2,1)} %q_ref.1, bf16[2048,512]{1,0:T(8,128)(2,1)} %get-tuple-element.9.mixed_ref, bf16[6,2048]{1,0:T(8,128)(2,1)} %reshape.6.halo_ref, f32[9,2048]{1,0:T(8,128)} %reshape.7.w_ref, f32[16,2048]{1,0:T(8,128)} %bitcast.6, f32[16,2048]{1,0:T(8,128)} %bitcast.7, ...), custom_call_target="tpu_custom_call" | custom-call | tf_op jit(solution)/shard_map/back/pallas_call | solution.py:319
Async XLA Ops:
  0.0 6.1 %copy-start = (f32[3,2048,3]{1,2,0:T(4,128)S(1)}, f32[3,2048,3]{1,2,0:T(4,128)}, u32[]{:S(2)}) copy-start(f32[3,2048,3]{1,2,0:T(4,128)} %param.13) | copy-start | bytes 221188
  2.7 6.6 %collective-permute-start = (bf16[3,2,2048]{2,1,0:T(2,128)(2,1)S(1)}, bf16[3,2,2048]{2,1,0:T(2,128)(2,1)S(1)}, u32[]{:S(2)}, u32[]{:S(2)}) collective-permute-start(bf16[3,2,2048]{2,1,0:T(2,128)(2,1)S(1)} %bitcast.9), channel_id=1, source_target_pairs={{0,4},{4,8},{8,12},{12,16},{16,20},{20,24},{24,28},{1,5},{5,9},{9,... | collective-permute-start | bytes 73736 | tf_op jit(solution)/shard_map/ppermute | solution.py:268

commit v4 on v3

--- a/solution.py
+++ b/solution.py
@@ -50,6 +50,9 @@
         sel[2 * i + 1, (2 * i) * 128] = 1
         sel[2 * i, (2 * i + 1) * 128] = 1
         sel[2 * i + 1, (2 * i + 1) * 128 + 1] = 1
+    pick = np.zeros((3, 8, 128))
+    for i in range(3):
+        pick[i, 2 * i, 126] = pick[i, 2 * i + 1, 127] = 1
     wide = np.kron(np.eye(9), np.ones((1, 128)))
     wide = np.concatenate([wide, np.zeros((7, 9 * 128))], axis=0)
     wide = np.concatenate([wide, wide], axis=0)
@@ -57,7 +60,7 @@
     b16 = lambda a: a.astype(jnp.bfloat16)
     return dict(
         fwd=b16(fwd), inv=b16(inv), spec=cat(sh, sh, sl), mom=cat(mh, ml),
-        car=cat(ch, ch, cl), sel=b16(sel), wide=b16(wide),
+        car=cat(ch, ch, cl), sel=b16(sel), pick=b16(pick), wide=b16(wide),
     )
 
 
@@ -81,9 +84,17 @@
     return jnp.concatenate([hi, lo], axis=0)
 
 
-def padded(m, count):
-    m = m.astype(jnp.float32)
-    return jnp.concatenate([m, jnp.zeros((count - m.shape[0], m.shape[1]), jnp.float32)], axis=0)
+def padded(ref, count):
+    parts = [ref[i] for i in range(3)]
+    return jnp.concatenate(parts + [jnp.zeros((count - 9, ref.shape[2]), jnp.float32)], axis=0)
+
+
+def last_two(p_ref, pick_ref, out_ref):
+    picked = [
+        lax.dot_general(pick_ref[i], p_ref[i], (((1,), (1,)), ((), ())), preferred_element_type=jnp.float32)
+        for i in range(3)
+    ]
+    out_ref[...] = (picked[0] + picked[1] + picked[2]).astype(out_ref.dtype)
 
 
 def series(decay, cheb_ref):
@@ -113,8 +124,8 @@
           mixed_ref, ends_ref, last_ref, power_ref,
           hr_ref, wide_w, cheb_ref):
     tile, length = p_ref.shape[1:]
-    hr_ref[...] = rowdot(padded(halo_ref[...], 8).astype(jnp.bfloat16), sel_ref[:, 256:])
-    wide_w[...] = rowdot(two(padded(w_ref[...], 16)), wide_ref[:, 384:])
+    hr_ref[...] = rowdot(halo_ref[...], sel_ref[:, 256:])
+    wide_w[...] = rowdot(two(padded(w_ref, 16)), wide_ref[:, 384:])
     series(decay_ref[...], cheb_ref)
 
     @pl.loop(0, tile // ROWS)
@@ -223,8 +234,8 @@
          sel_ref, wide_ref, fwd_ref, inv_ref, spec_ref, car_ref,
          out_ref, hr_ref, h_ref, y_ref, wide_w, cheb_ref):
     tile = mixed_ref.shape[0]
-    hr_ref[...] = rowdot(padded(halo_ref[...], 8).astype(jnp.bfloat16), sel_ref[:, :256])
-    wide_w[...] = rowdot(two(padded(w_ref[...], 16)), wide_ref[:, :384])
+    hr_ref[...] = rowdot(halo_ref[...], sel_ref[:, :256])
+    wide_w[...] = rowdot(two(padded(w_ref, 16)), wide_ref[:, :384])
     series(decay_ref[...], cheb_ref)
     step = jnp.exp(-BL * decay_ref[...])
     fold = 1.0 / (1.0 + step)
@@ -264,10 +275,18 @@
     tab = {k: jnp.asarray(v) for k, v in tables().items()}
     tile = math.gcd(512, channels)
     blocks = length // BL
-    tail = jnp.swapaxes(projected[:, :, length - 2 :], 1, 2)
+    taps = jnp.swapaxes(short_weight, 1, 2)
+    tail = pl.pallas_call(
+        last_two,
+        grid=(channels // tile,),
+        in_specs=[pl.BlockSpec((3, tile, 128), lambda i: (0, i, length // 128 - 1)),
+                  pl.BlockSpec((3, 8, 128), lambda i: (0, 0, 0))],
+        out_specs=pl.BlockSpec((8, tile), lambda i: (0, i)),
+        out_shape=jax.ShapeDtypeStruct((8, channels), jnp.bfloat16),
+        compiler_params=pltpu.CompilerParams(vmem_limit_bytes=56 * 2**20),
+        name="last_two",
+    )(projected, tab["pick"])
     halo = lax.ppermute(tail, "seq", [(i, i + 1) for i in range(n - 1)])
-    halo = halo.reshape(6, channels)
-    taps = jnp.swapaxes(short_weight, 1, 2).reshape(9, channels)
     decay, residue = decay_rates.T, residues.T
 
     full = lambda a: pl.BlockSpec(a.shape, lambda i: (0,) * a.ndim)
@@ -280,7 +299,7 @@
         front,
         grid=(count,),
         in_specs=[pl.BlockSpec((pl.Element(2), pl.Element(tile), pl.Element(length)), lambda i: (1, i * tile, 0)),
-                  lanes(6), lanes(9), lanes(16)] + [full(tab[k]) for k in names],
+                  lanes(8), pl.BlockSpec((3, 3, tile), lambda i: (0, 0, i)), lanes(16)] + [full(tab[k]) for k in names],
         out_specs=[rows, lanes(blocks * 16), lanes(16), lanes(16)],
         out_shape=[
             jax.ShapeDtypeStruct((channels, length), jnp.bfloat16),
@@ -319,7 +338,7 @@
     return pl.pallas_call(
         back,
         grid=(count,),
-        in_specs=[pl.BlockSpec((1, tile, length), lambda i: (0, i, 0)), rows, lanes(6), lanes(9), lanes(16),
+        in_specs=[pl.BlockSpec((1, tile, length), lambda i: (0, i, 0)), rows, lanes(8), pl.BlockSpec((3, 3, tile), lambda i: (0, 0, i)), lanes(16),
                   lanes(16), lanes(1), lanes(blocks * 16), lanes(16)] + [full(tab[k]) for k in names],
         out_specs=rows,
         out_shape=jax.ShapeDtypeStruct((channels, length), jnp.bfloat16),

time: 47 us -> 48.3 us (1.028)
  Pallas kernels: 36.9 us -> 40.6 us
  local copies, waits for them, and re-layouts: 3.96 us -> 0.61 us
  waiting for transfers between devices: 2.51 us -> 3.51 us
    pallas_call x0 -> x1, Pallas kernels: none -> 3.7 us  [shards(): pl.pallas_call(last_two, grid=(channels // tile,), in_specs=[pl.BlockSpec...]
    slice x1 -> x0, local copies, waits for them, and re-layouts: 1.93 us -> none  [shards(): tail = jnp.swapaxes(projected[:, :, length - 2:], 1, 2)]
    reshape x2 -> x0, local copies, waits for them, and re-layouts: 1.31 us -> none  [the longest x1 0.69 us: shards(): taps = jnp.swapaxes(short_weight, 1, 2).reshape(9, channels)]
    ppermute x1, waiting for transfers between devices: 2.51 us -> 3.51 us  [shards(): halo = lax.ppermute(tail, 'seq', [(i, i + 1) for i in range(n - 1)])]
  transfers between devices with their start and end apart: 1 -> 1, of which waited for: 1 -> 1; matrix products, arithmetic and copies ran while one was open for 1% -> 0% of each run, Pallas kernels for 0% -> 0%
where the time goes in v4:
time: 48.3 us; the launch traced here: 48.1 us
  Pallas kernels  40.6 us (84%)
  waiting for transfers between devices  3.51 us (7%)
  starting transfers between devices  3.39 us (7%)
  local copies, waits for them, and re-layouts  0.61 us (1%)
    pallas_call x1, Pallas kernels, shards(): pl.pallas_call(functools.partial(exchange, n), in_specs=[pl.BlockSpec(mem...  14 us
    pallas_call x1, Pallas kernels, shards(): pl.pallas_call(front, grid=(count,), in_specs=[pl.BlockSpec((pl.Element(2...  11.4 us
    pallas_call x1, Pallas kernels, shards(): pl.pallas_call(back, grid=(count,), in_specs=[pl.BlockSpec((1, tile, leng...  11.4 us
    pallas_call x1, Pallas kernels, shards(): pl.pallas_call(last_two, grid=(channels // tile,), in_specs=[pl.BlockSpec...  3.7 us
    ppermute x1, waiting for transfers between devices, shards(): halo = lax.ppermute(tail, 'seq', [(i, i + 1) for i in range(n - 1)])  3.51 us
    ppermute x1, starting transfers between devices, shards(): halo = lax.ppermute(tail, 'seq', [(i, i + 1) for i in range(n - 1)])  3.39 us
  transfers between devices with their start and end apart: 1, of which 1 were waited for; matrix products, arithmetic and copies ran while one was open for 0% of the time, Pallas kernels for 0%

profile of v4, /device:TPU:28, one launch (start us, length us, event | category | flops | bytes accessed | tf_op | source)
XLA Modules:
  0.0 48.1 jit_solution(14340453340935394239)
XLA Ops:
  0.0 3.7 %last_two.1 = bf16[8,2048]{1,0:T(8,128)(2,1)} custom-call(bf16[3,2048,512]{2,1,0:T(8,128)(2,1)} %q_ref.1, bf16[3,8,128]{2,1,0:T(8,128)(2,1)} %constant.22.clone.pick_ref), custom_call_target="tpu_custom_call" | custom-call | tf_op jit(solution)/shard_map/last_two/pallas_call | solution.py:279
  3.7 3.4 %collective-permute-start = (bf16[8,2048]{1,0:T(8,128)(2,1)}, bf16[8,2048]{1,0:T(8,128)(2,1)S(1)}, u32[]{:S(2)}, u32[]{:S(2)}) collective-permute-start(bf16[8,2048]{1,0:T(8,128)(2,1)} %last_two.1), channel_id=1, source_target_pairs={{0,4},{4,8},{8,12},{12,16},{16,20},{20,24},{24,28},{1,5},{5,9},{9,... | collective-permute-start | bytes 98312 | tf_op jit(solution)/shard_map/ppermute | solution.py:289
  7.1 3.5 %collective-permute-done.halo_ref = bf16[8,2048]{1,0:T(8,128)(2,1)S(1)} collective-permute-done((bf16[8,2048]{1,0:T(8,128)(2,1)}, bf16[8,2048]{1,0:T(8,128)(2,1)S(1)}, u32[]{:S(2)}, u32[]{:S(2)}) %collective-permute-start) | collective-permute-done | bytes 32800 | tf_op jit(solution)/shard_map/ppermute | solution.py:289
  10.6 0.0 copy-start
  10.6 0.6 %copy-done = bf16[8,2048]{1,0:T(8,128)(2,1)} copy-done((bf16[8,2048]{1,0:T(8,128)(2,1)}, bf16[8,2048]{1,0:T(8,128)(2,1)S(1)}, u32[]{:S(2)}) %copy-start) | copy-done | bytes 32792
  11.2 11.4 %front.1 = (bf16[2048,512]{1,0:T(8,128)(2,1)}, f32[64,2048]{1,0:T(8,128)}, bf16[16,2048]{1,0:T(8,128)(2,1)}, f32[16,2048]{1,0:T(8,128)}) custom-call(bf16[3,2048,512]{2,1,0:T(8,128)(2,1)} %q_ref.1, bf16[8,2048]{1,0:T(8,128)(2,1)} %copy-done, f32[3,3,2048]{2,1,0:T(4,128)} %bitcast.6, f32[16,2048]{1,0:T(8,128)} %bitcast.4, ...), custom_call_target="tpu_custom_call" | custom-call | tf_op jit(solution)/shard_map/front/pallas_call | solution.py:298
  22.7 14.0 %exchange.1.init_ref = f32[16,2048]{1,0:T(8,128)} custom-call(bf16[16,2048]{1,0:T(8,128)(2,1)} %get-tuple-element.11.last_ref, f32[16,2048]{1,0:T(8,128)} %get-tuple-element.12.power_ref), custom_call_target="tpu_custom_call" | custom-call | tf_op jit(solution)/shard_map/exchange/pallas_call | solution.py:318
  36.7 11.4 %back.1 = bf16[2048,512]{1,0:T(8,128)(2,1)} custom-call(bf16[3,2048,512]{2,1,0:T(8,128)(2,1)} %q_ref.1, bf16[2048,512]{1,0:T(8,128)(2,1)} %get-tuple-element.9.mixed_ref, bf16[8,2048]{1,0:T(8,128)(2,1)} %copy-done, f32[3,3,2048]{2,1,0:T(4,128)} %bitcast.7, f32[16,2048]{1,0:T(8,128)} %bitcast.5, f32[16,2048]{1,0:T(8,128)} %bitcast.8, f32[1,2048]{1,0:T(1,128)} %bitcast.9, ...), custom_call_target="tpu_custom_call" | custom-call | tf_op jit(solution)/shard_map/back/pallas_call | solution.py:338
Async XLA Ops:
  3.7 6.9 %collective-permute-start = (bf16[8,2048]{1,0:T(8,128)(2,1)}, bf16[8,2048]{1,0:T(8,128)(2,1)S(1)}, u32[]{:S(2)}, u32[]{:S(2)}) collective-permute-start(bf16[8,2048]{1,0:T(8,128)(2,1)} %last_two.1), channel_id=1, source_target_pairs={{0,4},{4,8},{8,12},{12,16},{16,20},{20,24},{24,28},{1,5},{5,9},{9,... | collective-permute-start | bytes 98312 | tf_op jit(solution)/shard_map/ppermute | solution.py:289
  10.6 0.6 %copy-start = (bf16[8,2048]{1,0:T(8,128)(2,1)}, bf16[8,2048]{1,0:T(8,128)(2,1)S(1)}, u32[]{:S(2)}) copy-start(bf16[8,2048]{1,0:T(8,128)(2,1)S(1)} %collective-permute-done.halo_ref) | copy-start | bytes 98308

commit v5 on v3

--- a/solution.py
+++ b/solution.py
@@ -81,9 +81,10 @@
     return jnp.concatenate([hi, lo], axis=0)
 
 
-def padded(m, count):
-    m = m.astype(jnp.float32)
-    return jnp.concatenate([m, jnp.zeros((count - m.shape[0], m.shape[1]), jnp.float32)], axis=0)
+def padded(ref, count):
+    parts = [ref[i].astype(jnp.float32) for i in range(3)]
+    rest = count - 3 * ref.shape[1]
+    return jnp.concatenate(parts + [jnp.zeros((rest, ref.shape[2]), jnp.float32)], axis=0)
 
 
 def series(decay, cheb_ref):
@@ -113,8 +114,8 @@
           mixed_ref, ends_ref, last_ref, power_ref,
           hr_ref, wide_w, cheb_ref):
     tile, length = p_ref.shape[1:]
-    hr_ref[...] = rowdot(padded(halo_ref[...], 8).astype(jnp.bfloat16), sel_ref[:, 256:])
-    wide_w[...] = rowdot(two(padded(w_ref[...], 16)), wide_ref[:, 384:])
+    hr_ref[...] = rowdot(padded(halo_ref, 8).astype(jnp.bfloat16), sel_ref[:, 256:])
+    wide_w[...] = rowdot(two(padded(w_ref, 16)), wide_ref[:, 384:])
     series(decay_ref[...], cheb_ref)
 
     @pl.loop(0, tile // ROWS)
@@ -223,8 +224,8 @@
          sel_ref, wide_ref, fwd_ref, inv_ref, spec_ref, car_ref,
          out_ref, hr_ref, h_ref, y_ref, wide_w, cheb_ref):
     tile = mixed_ref.shape[0]
-    hr_ref[...] = rowdot(padded(halo_ref[...], 8).astype(jnp.bfloat16), sel_ref[:, :256])
-    wide_w[...] = rowdot(two(padded(w_ref[...], 16)), wide_ref[:, :384])
+    hr_ref[...] = rowdot(padded(halo_ref, 8).astype(jnp.bfloat16), sel_ref[:, :256])
+    wide_w[...] = rowdot(two(padded(w_ref, 16)), wide_ref[:, :384])
     series(decay_ref[...], cheb_ref)
     step = jnp.exp(-BL * decay_ref[...])
     fold = 1.0 / (1.0 + step)
@@ -264,12 +265,12 @@
     tab = {k: jnp.asarray(v) for k, v in tables().items()}
     tile = math.gcd(512, channels)
     blocks = length // BL
+    taps = jnp.swapaxes(short_weight, 1, 2)
     tail = jnp.swapaxes(projected[:, :, length - 2 :], 1, 2)
     halo = lax.ppermute(tail, "seq", [(i, i + 1) for i in range(n - 1)])
-    halo = halo.reshape(6, channels)
-    taps = jnp.swapaxes(short_weight, 1, 2).reshape(9, channels)
     decay, residue = decay_rates.T, residues.T
 
+    streams = lambda r: pl.BlockSpec((3, r, tile), lambda i: (0, 0, i))
     full = lambda a: pl.BlockSpec(a.shape, lambda i: (0,) * a.ndim)
     lanes = lambda r: pl.BlockSpec((r, tile), lambda i: (0, i))
     rows = pl.BlockSpec((tile, length), lambda i: (i, 0))
@@ -280,7 +281,7 @@
         front,
         grid=(count,),
         in_specs=[pl.BlockSpec((pl.Element(2), pl.Element(tile), pl.Element(length)), lambda i: (1, i * tile, 0)),
-                  lanes(6), lanes(9), lanes(16)] + [full(tab[k]) for k in names],
+                  streams(2), streams(3), lanes(16)] + [full(tab[k]) for k in names],
         out_specs=[rows, lanes(blocks * 16), lanes(16), lanes(16)],
         out_shape=[
             jax.ShapeDtypeStruct((channels, length), jnp.bfloat16),
@@ -319,7 +320,7 @@
     return pl.pallas_call(
         back,
         grid=(count,),
-        in_specs=[pl.BlockSpec((1, tile, length), lambda i: (0, i, 0)), rows, lanes(6), lanes(9), lanes(16),
+        in_specs=[pl.BlockSpec((1, tile, length), lambda i: (0, i, 0)), rows, streams(2), streams(3), lanes(16),
                   lanes(16), lanes(1), lanes(blocks * 16), lanes(16)] + [full(tab[k]) for k in names],
         out_specs=rows,
         out_shape=jax.ShapeDtypeStruct((channels, length), jnp.bfloat16),

time: 47 us -> 47 us (level)
  local copies, waits for them, and re-layouts: 3.96 us -> 3.23 us
  waiting for transfers between devices: 2.51 us -> 3.21 us
    reshape x2 -> x0, local copies, waits for them, and re-layouts: 1.31 us -> none  [the longest x1 0.69 us: shards(): taps = jnp.swapaxes(short_weight, 1, 2).reshape(9, channels)]
    ppermute x1, waiting for transfers between devices: 2.51 us -> 3.21 us  [shards(): halo = lax.ppermute(tail, 'seq', [(i, i + 1) for i in range(n - 1)])]
    unnamed x3, local copies, waits for them, and re-layouts: 0.72 us -> 1.33 us
  transfers between devices with their start and end apart: 1 -> 1, of which waited for: 1 -> 1; matrix products, arithmetic and copies ran while one was open for 1% -> 0% of each run, Pallas kernels for 0% -> 0%
where the time goes in v5:
time: 47 us; the launch traced here: 46.8 us
  Pallas kernels  36.9 us (79%)
  starting transfers between devices  3.4 us (7%)
  local copies, waits for them, and re-layouts  3.23 us (7%)
  waiting for transfers between devices  3.21 us (7%)
    pallas_call x1, Pallas kernels, shards(): pl.pallas_call(functools.partial(exchange, n), in_specs=[pl.BlockSpec(mem...  14 us
    pallas_call x1, Pallas kernels, shards(): pl.pallas_call(front, grid=(count,), in_specs=[pl.BlockSpec((pl.Element(2...  11.5 us
    pallas_call x1, Pallas kernels, shards(): pl.pallas_call(back, grid=(count,), in_specs=[pl.BlockSpec((1, tile, leng...  11.4 us
    ppermute x1, starting transfers between devices, shards(): halo = lax.ppermute(tail, 'seq', [(i, i + 1) for i in range(n - 1)])  3.4 us
    ppermute x1, waiting for transfers between devices, shards(): halo = lax.ppermute(tail, 'seq', [(i, i + 1) for i in range(n - 1)])  3.21 us
    slice x1, local copies, waits for them, and re-layouts, shards(): tail = jnp.swapaxes(projected[:, :, length - 2:], 1, 2)  1.9 us
    unnamed x3, local copies, waits for them, and re-layouts  1.33 us
  transfers between devices with their start and end apart: 1, of which 1 were waited for; matrix products, arithmetic and copies ran while one was open for 0% of the time, Pallas kernels for 0%

profile of v5, /device:TPU:28, one launch (start us, length us, event | category | flops | bytes accessed | tf_op | source)
XLA Modules:
  0.0 46.8 jit_solution(15060069699252071100)
XLA Ops:
  0.0 1.9 %slice.3 = bf16[3,2048,2]{2,1,0:T(8,128)(2,1)S(1)} slice(bf16[3,2048,512]{2,1,0:T(8,128)(2,1)} %q_ref.1), slice={[0:3], [0:2048], [510:512]} | slice | bytes 49152 | tf_op jit(solution)/shard_map/slice | solution.py:269
  1.9 0.7 %copy.14 = bf16[3,2048,2]{1,2,0:T(2,128)(2,1)S(1)} copy(bf16[3,2048,2]{2,1,0:T(8,128)(2,1)S(1)} %slice.3) | data formatting | bytes 49152
  2.6 3.4 %collective-permute-start = (bf16[3,2,2048]{2,1,0:T(2,128)(2,1)S(1)}, bf16[3,2,2048]{2,1,0:T(2,128)(2,1)S(1)}, u32[]{:S(2)}, u32[]{:S(2)}) collective-permute-start(bf16[3,2,2048]{2,1,0:T(2,128)(2,1)S(1)} %bitcast.10), channel_id=1, source_target_pairs={{0,4},{4,8},{8,12},{12,16},{16,20},{20,24},{24,28},{1,5},{5,9},{9,... | collective-permute-start | bytes 73736 | tf_op jit(solution)/shard_map/ppermute | solution.py:270
  6.0 3.2 %collective-permute-done.halo_ref = bf16[3,2,2048]{2,1,0:T(2,128)(2,1)S(1)} collective-permute-done((bf16[3,2,2048]{2,1,0:T(2,128)(2,1)S(1)}, bf16[3,2,2048]{2,1,0:T(2,128)(2,1)S(1)}, u32[]{:S(2)}, u32[]{:S(2)}) %collective-permute-start) | collective-permute-done | bytes 24608 | tf_op jit(solution)/shard_map/ppermute | solution.py:270
  9.2 0.0 copy-start
  9.2 0.6 %copy-done = bf16[3,2,2048]{2,1,0:T(2,128)(2,1)} copy-done((bf16[3,2,2048]{2,1,0:T(2,128)(2,1)}, bf16[3,2,2048]{2,1,0:T(2,128)(2,1)S(1)}, u32[]{:S(2)}) %copy-start) | copy-done | bytes 24600
  9.8 11.5 %front.1 = (bf16[2048,512]{1,0:T(8,128)(2,1)}, f32[64,2048]{1,0:T(8,128)}, bf16[16,2048]{1,0:T(8,128)(2,1)}, f32[16,2048]{1,0:T(8,128)}) custom-call(bf16[3,2048,512]{2,1,0:T(8,128)(2,1)} %q_ref.1, bf16[3,2,2048]{2,1,0:T(2,128)(2,1)} %copy-done, f32[3,3,2048]{2,1,0:T(4,128)} %bitcast.7, f32[16,2048]{1,0:T(8,128)} %bitcast.5, ...), custom_call_target="tpu_custom_call" | custom-call | tf_op jit(solution)/shard_map/front/pallas_call | solution.py:280
  21.3 14.0 %exchange.1.init_ref = f32[16,2048]{1,0:T(8,128)} custom-call(bf16[16,2048]{1,0:T(8,128)(2,1)} %get-tuple-element.11.last_ref, f32[16,2048]{1,0:T(8,128)} %get-tuple-element.12.power_ref), custom_call_target="tpu_custom_call" | custom-call | tf_op jit(solution)/shard_map/exchange/pallas_call | solution.py:300
  35.4 11.4 %back.1 = bf16[2048,512]{1,0:T(8,128)(2,1)} custom-call(bf16[3,2048,512]{2,1,0:T(8,128)(2,1)} %q_ref.1, bf16[2048,512]{1,0:T(8,128)(2,1)} %get-tuple-element.9.mixed_ref, bf16[3,2,2048]{2,1,0:T(2,128)(2,1)} %copy-done, f32[3,3,2048]{2,1,0:T(4,128)} %bitcast.8, f32[16,2048]{1,0:T(8,128)} %bitcast.6, f32[16,2048]{1,0:T(8,128)} %bitcast.9, f32[1,2048]{1,0:T(1,128)} %bitcast.11, ...), custom_call_target="tpu_custom_call" | custom-call | tf_op jit(solution)/shard_map/back/pallas_call | solution.py:320
Async XLA Ops:
  2.6 6.6 %collective-permute-start = (bf16[3,2,2048]{2,1,0:T(2,128)(2,1)S(1)}, bf16[3,2,2048]{2,1,0:T(2,128)(2,1)S(1)}, u32[]{:S(2)}, u32[]{:S(2)}) collective-permute-start(bf16[3,2,2048]{2,1,0:T(2,128)(2,1)S(1)} %bitcast.10), channel_id=1, source_target_pairs={{0,4},{4,8},{8,12},{12,16},{16,20},{20,24},{24,28},{1,5},{5,9},{9,... | collective-permute-start | bytes 73736 | tf_op jit(solution)/shard_map/ppermute | solution.py:270
  9.2 0.6 %copy-start = (bf16[3,2,2048]{2,1,0:T(2,128)(2,1)}, bf16[3,2,2048]{2,1,0:T(2,128)(2,1)S(1)}, u32[]{:S(2)}) copy-start(bf16[3,2,2048]{2,1,0:T(2,128)(2,1)S(1)} %collective-permute-done.halo_ref) | copy-start | bytes 73732
